TPU v7x, 256 devices: a whole 4x4x8 slice. The times are simulated.
256 devices in a mesh: section: 2 (over core), item: 128 (over y, x, z).
Axes of the slice: x: 4, y: 4, z: 8, core: 2. Of those that a mesh axis runs over, the one named last changes fastest.
Arguments:
- history: bfloat16 [128, 1024, 1024], P('item', 'section'), may hold values from -12 to 12
- hist_len: int32 [128], P('item'), may hold values from 16 to 1024
- cand_ids: int32 [128, 768], P('item', 'section'), may hold values from 0 to 524287, as said below
- cand_count: int32 [128], P('item'), may hold values from 192 to 768
- table: bfloat16 [524288, 512], P('item'), may hold values from -6 to 6
- w_event: bfloat16 [1024, 1024], replicated, may hold values from -0.1875 to 0.1875
- w_kv: bfloat16 [1024, 1024], replicated, may hold values from -0.1875 to 0.1875
- pool_query: bfloat16 [1024], replicated, may hold values from -8 to 8
- w_rank: bfloat16 [2048, 512], replicated, may hold values from -0.125 to 0.125
- w_out: float32 [512], replicated, may hold values from -0.25 to 0.25
Outputs:
- scores: float32 [128, 768], P('item', 'section')
- user_state: bfloat16 [128, 1024], P('item')
Inputs may be any that keep to these rules, and one draw needn't show every extreme that they name: `cand_ids`: every id is a row of the table; its owner is id // 4096. Among the 384 slots that one device holds (its requests' half of the candidate slots), at most 6 ids have the same owner, and in every device's slots one owner has exactly 6.
All inputs are finite; a program needn't handle non-finite values.
Results may differ from a plain program's by a relative error of at most 0.025.
Values may be sent and summed in bfloat16 or wider, within the bound.
A program may use at most 64 MiB of HBM per device.

v0:
```python
import math

import jax
import jax.numpy as jnp
from jax import lax
from jax.sharding import PartitionSpec as P

HEAD = 128


masked_value = -1e30


def merged(x, axis, combine):
    everything = jax.tree.map(lambda part: lax.all_gather(part, axis), x)
    initial = jax.tree.map(lambda part: part[0], everything)

    def hop(k, so_far):
        return combine(so_far, jax.tree.map(lambda part: part[k], everything))

    return lax.fori_loop(1, lax.axis_size(axis), hop, initial)


def combine_soft(first, second):
    first_max, first_sum = first
    second_max, second_sum = second
    joint_max = jnp.maximum(first_max, second_max)
    joint_sum = first_sum * jnp.exp(first_max - joint_max) + second_sum * jnp.exp(
        second_max - joint_max
    )
    return (joint_max, joint_sum)


def on_device(
    history, hist_len, cand_ids, cand_count, table, w_event, w_kv, pool_query, w_rank, w_out
):
    requests, half_len, model_width = history.shape
    item_width = table.shape[1]
    rows_local = table.shape[0]
    pool_heads = model_width // HEAD
    target_heads = item_width // HEAD
    score_scale = 1.0 / math.sqrt(HEAD)
    section_index = lax.axis_index("section")
    owner_count = lax.axis_size("item")
    pre_act = jnp.einsum("rtd,de->rte", history, w_event, preferred_element_type=jnp.float32)
    states = (history.astype(jnp.float32) + jax.nn.gelu(pre_act)).astype(jnp.bfloat16)
    key_value = jnp.einsum("rtd,de->rte", states, w_kv, preferred_element_type=jnp.float32).astype(
        jnp.bfloat16
    )
    local_events = section_index * half_len + jnp.arange(half_len)
    local_mask = local_events[None, :] < hist_len[:, None]
    split_heads = states.reshape(requests, half_len, pool_heads, HEAD)
    pool_score = (
        jnp.einsum(
            "rthc,hc->rht",
            split_heads,
            pool_query.reshape(pool_heads, HEAD),
            preferred_element_type=jnp.float32,
        )
        * score_scale
    )
    pool_score = jnp.where(local_mask[:, None, :], pool_score, masked_value)
    row_max = jnp.max(pool_score, axis=-1)
    row_sum = jnp.sum(jnp.exp(pool_score - row_max[..., None]), axis=-1)
    row_max, row_sum = merged((row_max, row_sum), "section", combine_soft)
    pool_weight = (jnp.exp(pool_score - row_max[..., None]) / row_sum[..., None]).astype(
        jnp.bfloat16
    )
    pooled_part = jnp.einsum(
        "rht,rthc->rhc", pool_weight, split_heads, preferred_element_type=jnp.float32
    )
    pooled = lax.psum(pooled_part, "section")
    user_state = pooled.reshape(requests, model_width).astype(jnp.bfloat16)
    slot_half = cand_ids.shape[1]
    slot_total = requests * slot_half
    bucket_cap = 2 * slot_total // owner_count
    cand_flat = cand_ids.reshape(slot_total)
    owner_ids = cand_flat // rows_local
    offsets = cand_flat - owner_ids * rows_local
    owner_onehot = (owner_ids[:, None] == jnp.arange(owner_count)[None, :]).astype(jnp.float32)
    lower_ones = jnp.tril(jnp.ones((slot_total, slot_total), jnp.float32), -1)
    earlier = jnp.dot(lower_ones, owner_onehot, precision=lax.Precision.HIGHEST)
    rank_in_owner = jnp.sum(earlier * owner_onehot, axis=1).astype(jnp.int32)
    slot_index = owner_ids * bucket_cap + rank_in_owner
    buckets = jnp.zeros((owner_count * bucket_cap,), jnp.int32).at[slot_index].set(offsets)
    buckets = buckets.reshape(owner_count, bucket_cap)
    looked_up = jnp.take(
        table, lax.all_to_all(buckets, "item", split_axis=0, concat_axis=0, tiled=True), axis=0
    )
    returned = lax.all_to_all(looked_up, "item", split_axis=0, concat_axis=0, tiled=True)
    cand_rows = returned.reshape(owner_count * bucket_cap, item_width)[slot_index]
    cand_rows = cand_rows.reshape(requests, slot_half, item_width)
    whole_kv = lax.all_gather(key_value, "section", axis=1, tiled=True)
    event_total = whole_kv.shape[1]
    whole_mask = jnp.arange(event_total)[None, :] < hist_len[:, None]
    key_part = whole_kv[:, :, :item_width].reshape(requests, event_total, target_heads, HEAD)
    value_part = whole_kv[:, :, item_width:].reshape(requests, event_total, target_heads, HEAD)
    target_score = (
        jnp.einsum(
            "rjhc,rthc->rjht",
            cand_rows.reshape(requests, slot_half, target_heads, HEAD),
            key_part,
            preferred_element_type=jnp.float32,
        )
        * score_scale
    )
    target_score = jnp.where(whole_mask[:, None, None, :], target_score, masked_value)
    target_max = jnp.max(target_score, axis=-1, keepdims=True)
    target_exp = jnp.exp(target_score - target_max)
    target_weight = (target_exp / jnp.sum(target_exp, axis=-1, keepdims=True)).astype(jnp.bfloat16)
    attended_heads = jnp.zeros((requests, slot_half, target_heads, HEAD), jnp.float32)
    for half_number in range(event_total // half_len):
        first = half_number * half_len
        half_term = jnp.einsum(
            "rjht,rthc->rjhc",
            target_weight[:, :, :, first : first + half_len],
            value_part[:, first : first + half_len],
            preferred_element_type=jnp.float32,
        )
        attended_heads = attended_heads + half_term.astype(jnp.bfloat16).astype(jnp.float32)
    attended = attended_heads.reshape(requests, slot_half, item_width).astype(jnp.bfloat16)
    pre_rank = jnp.einsum(
        "rje,ef->rjf", cand_rows, w_rank[:item_width], preferred_element_type=jnp.float32
    )
    pre_rank = pre_rank + jnp.einsum(
        "rje,ef->rjf",
        attended,
        w_rank[item_width : 2 * item_width],
        preferred_element_type=jnp.float32,
    )
    user_term = jnp.dot(user_state, w_rank[2 * item_width :], preferred_element_type=jnp.float32)
    rank_hidden = jax.nn.relu(pre_rank + user_term[:, None, :])
    cand_score = jnp.einsum("rjf,f->rj", rank_hidden, w_out, precision=lax.Precision.HIGHEST)
    slot_number = section_index * slot_half + jnp.arange(slot_half)
    live_mask = slot_number[None, :] < cand_count[:, None]
    scores = jnp.where(live_mask, cand_score, jnp.zeros_like(cand_score))
    return (scores, user_state)


def solution(mesh):
    placed = (
        P("item", "section", None),
        P("item"),
        P("item", "section"),
        P("item"),
        P("item", None),
        P(),
        P(),
        P(),
        P(),
        P(),
    )
    return jax.shard_map(
        on_device,
        mesh=mesh,
        in_specs=placed,
        out_specs=(P("item", "section"), P("item", None)),
        check_vma=False,
    )
```

profile of v0, /device:TPU:1, one launch (start us, length us, event | category | flops | bytes accessed | tf_op | source)
XLA Modules:
  0.0 120.6 jit_solution(937562578468070721)
XLA Ops:
  7.2 0.0 copy-start
  7.2 0.8 reduce.6
  8.0 0.6 fusion.22
  8.7 0.7 fusion.56
  9.4 2.9 %scatter_custom_fusion = s32[768]{0:T(1024)S(1)} fusion(s32[384]{0:T(512)S(1)} %fusion.56, s32[384]{0:T(512)S(1)} %get-tuple-element.26, s32[]{:T(128)} %constant.31.clone.1), kind=kCustom, calls=%fused_computation.92 | custom fusion | bytes 3076 | tf_op jit(solution)/shard_map/scatter | solution.py:85
  12.3 0.8 all_to_all.13
  13.1 16.3 %all-to-all-start = ((s32[128,1,6]{2,1,0:T(1,128)}), s32[128,1,6]{2,1,0:T(1,128)S(1)}, u32[]{:S(2)}, u32[]{:S(2)}) async-start(s32[128,1,6]{2,1,0:T(1,128)} %bitcast.2), calls=%async_computation | async-start | bytes 131072 | tf_op jit(solution)/shard_map/all_to_all | solution.py:88
  29.4 0.0 all-gather.5.cloned.1.call-start
  29.5 0.0 copy-start.4
  29.5 3.5 %fusion.11 = bf16[1,512,1024]{2,1,0:T(8,128)(2,1)S(1)} fusion(bf16[1,512,1024]{2,1,0:T(8,128)(2,1)} %param.10, bf16[1024,1024]{1,0:T(8,128)(2,1)S(1)} %copy-done), kind=kOutput, calls=%fused_computation.19 | convolution fusion | flops 1079508992 | bytes 4194304 | tf_op jit(solution)/shard_map/rtd,de->rte/dot_general | solution.py:45
  33.0 2.3 %convolution_convert_fusion = bf16[512,1024]{1,0:T(8,128)(2,1)} fusion(bf16[1024,1024]{1,0:T(8,128)(2,1)S(1)} %copy-done.4, bf16[1,512,1024]{2,1,0:T(8,128)(2,1)S(1)} %fusion.11), kind=kOutput, calls=%fused_computation.24 | convolution fusion | flops 1074266112 | bytes 4194304 | tf_op jit(solution)/shard_map/rtd,de->rte/dot_general | solution.py:47
  35.2 0.0 all-gather.5.cloned.1.call-update
  35.2 1.3 %copy.47 = bf16[64,8,8,128]{3,2,1,0:T(8,128)(2,1)} copy(bf16[64,8,8,128]{3,1,2,0:T(8,128)(2,1)S(1)} %bitcast.141) | data formatting | bytes 2097152
  36.5 3.5 %all-to-all-done = s32[128,1,6]{2,1,0:T(1,128)S(1)} async-done(((s32[128,1,6]{2,1,0:T(1,128)}), s32[128,1,6]{2,1,0:T(1,128)S(1)}, u32[]{:S(2)}, u32[]{:S(2)}) %all-to-all-start) | async-done | bytes 3104 | tf_op jit(solution)/shard_map/all_to_all | solution.py:88
  40.0 0.1 reshape.392
  40.1 5.4 %gather_fusion = bf16[768,512]{1,0:T(8,128)(2,1)S(1)} fusion(bf16[4096,512]{1,0:T(8,128)(2,1)} %param.14, s32[1024]{0:T(1024)S(1)} %pad_clamp_fusion.1), kind=kCustom, calls=%fused_computation | custom fusion | bytes 1575936 | tf_op jit(solution)/shard_map/jit(_take)/gather | solution.py:87
  45.6 1.3 %reshape.391 = bf16[128,6,512]{2,1,0:T(8,128)(2,1)} reshape(bf16[768,512]{1,0:T(8,128)(2,1)S(1)} %gather_fusion) | data formatting | bytes 1572864 | tf_op jit(solution)/shard_map/jit(_take)/gather | solution.py:87
  46.9 0.0 copy-start.5
  46.9 2.6 %broadcast_select_fusion = bf16[128,6,512]{2,1,0:T(8,128)(2,1)} fusion(bf16[128,6,512]{2,1,0:T(8,128)(2,1)} %reshape.391, pred[128,6]{1,0:T(8,128)(4,1)S(1)} %compare_and_fusion), kind=kLoop, calls=%fused_computation.44 | loop fusion | flops 393216 | bytes 1573632 | tf_op jit(solution)/shard_map/jit(_take)/select_n | solution.py:87
  49.5 10.4 %all-to-all-start.1 = ((bf16[128,6,512]{2,1,0:T(8,128)(2,1)}), bf16[128,6,512]{2,1,0:T(8,128)(2,1)}, u32[]{:S(2)}, u32[]{:S(2)}) async-start(bf16[128,6,512]{2,1,0:T(8,128)(2,1)} %broadcast_select_fusion), calls=%async_computation.1 | async-start | bytes 2097152 | tf_op jit(solution)/shard_map/all_to_all | solution.py:90
  59.9 0.4 fusion.34
  61.0 0.6 dynamic-slice
  62.2 0.1 fusion.48
  62.4 0.2 dynamic-update-slice
  62.6 0.2 exponential_reduce_fusion
  62.8 0.2 dynamic-update-slice.1
  63.0 3.6 %all-reduce.2 = (f32[16]{0:T(128)S(1)}, f32[16]{0:T(128)S(1)}) all-reduce(f32[16]{0:T(128)S(1)} %dynamic-update-slice.1, f32[16]{0:T(128)S(1)} %dynamic-update-slice), channel_id=4, replica_groups=mesh['section'=2,'item'=128] {'section'}, use_global_device_ids=true, to_apply=%add.1 | all-reduce | flops 32 | bytes 256
  66.7 0.1 fusion.57
  66.7 0.1 fusion.49
  66.8 0.3 fusion.32
  67.1 2.6 %psum.7 = bf16[1,8,128]{2,1,0:T(8,128)(2,1)S(1)} all-reduce(f32[1,8,128]{2,1,0:T(8,128)S(1)} %bitcast.148), channel_id=1, replica_groups=mesh['section'=2,'item'=128] {'section'}, use_global_device_ids=true, to_apply=%region_6.7 | all-reduce | flops 1024 | bytes 6144 | tf_op jit(solution)/shard_map/psum | solution.py:72
  70.4 0.6 copy.77
  71.0 1.5 %fusion.30 = f32[1,512]{1,0:T(1,128)S(1)} fusion(bf16[1024,1]{0,1:T(2,128)(2,1)S(1)} %reshape.440, bf16[2048,512]{1,0:T(8,128)(2,1)} %param.18), kind=kOutput, calls=%fused_computation.42 | convolution fusion | flops 1048576 | bytes 1052672 | tf_op jit(solution)/shard_map/dot_general | solution.py:131
  72.5 16.3 %all-to-all-done.1 = bf16[128,6,512]{2,1,0:T(8,128)(2,1)} async-done(((bf16[128,6,512]{2,1,0:T(8,128)(2,1)}), bf16[128,6,512]{2,1,0:T(8,128)(2,1)}, u32[]{:S(2)}, u32[]{:S(2)}) %all-to-all-start.1) | async-done | bytes 786464 | tf_op jit(solution)/shard_map/all_to_all | solution.py:90
  88.8 1.4 %reshape.378 = bf16[768,512]{1,0:T(8,128)(2,1)S(1)} reshape(bf16[128,6,512]{2,1,0:T(8,128)(2,1)} %all-to-all-done.1) | data formatting | bytes 1572864 | tf_op jit(solution)/shard_map/reshape | solution.py:91
  90.2 2.1 %gather_fusion.1 = bf16[384,512]{1,0:T(8,128)(2,1)S(1)} fusion(bf16[768,512]{1,0:T(8,128)(2,1)S(1)} %reshape.378, s32[1024]{0:T(1024)S(1)} %pad_clamp_fusion), kind=kCustom, calls=%fused_computation.1 | custom fusion | bytes 787968 | tf_op jit(solution)/shard_map/gather | solution.py:91
  92.3 2.3 %fusion.38 = f32[384,512]{1,0:T(8,128)} fusion(bf16[384,512]{1,0:T(8,128)(2,1)S(1)} %gather_fusion.1, bf16[2048,512]{1,0:T(8,128)(2,1)} %param.18), kind=kOutput, calls=%fused_computation.54 | convolution fusion | flops 201326592 | bytes 1703936 | tf_op jit(solution)/shard_map/rje,ef->rjf/dot_general | solution.py:122
  94.6 2.7 %fusion.60 = (bf16[1,1024,512]{2,1,0:T(8,128)(2,1)}, bf16[1,1024,512]{2,1,0:T(8,128)(2,1)S(1)}) fusion(bf16[1,1024,1024]{2,1,0:T(8,128)(2,1)} %bitcast.137), kind=kLoop, calls=%fused_computation.107 | loop fusion | bytes 4194304 | tf_op jit(solution)/shard_map/slice | solution.py:97
  97.2 1.1 reshape.383
  98.3 2.4 %bitcast_reduce_fusion = (f32[384,4]{0,1:T(4,128)S(1)}, f32[4,1024,384]{2,1,0:T(8,128)S(1)}) fusion(pred[1024]{0:T(1024)(128)(4,1)S(1)} %iota_compare_fusion.4, bf16[1024,4,128]{2,1,0:T(4,128)(2,1)} %reshape.383, bf16[384,512]{1,0:T(8,128)(2,1)S(1)} %gather_fusion.1), kind=kOutput, calls=%fused_computation.4 | convolution fusion | flops 407370240 | bytes 7740416 | tf_op jit(solution)/shard_map/rjhc,rthc->rjht/dot_general | solution.py:99
  100.8 1.8 %fusion.1 = f32[384,4]{0,1:T(4,128)S(1)} fusion(f32[4,1024,384]{2,1,0:T(8,128)S(1)} %get-tuple-element.29, f32[384,4]{0,1:T(4,128)S(1)} %get-tuple-element.28, pred[1024]{0:T(1024)(128)(4,1)S(1)} %iota_compare_fusion.4), kind=kLoop, calls=%fused_computation.8 | loop fusion | flops 6289920 | bytes 6304768 | tf_op jit(solution)/shard_map/reduce_sum | solution.py:110
  102.5 3.1 %divide_convert_fusion = bf16[1,384,4,1024]{1,3,2,0:T(8,128)(2,1)} fusion(f32[4,1024,384]{2,1,0:T(8,128)S(1)} %get-tuple-element.29, f32[384,4]{0,1:T(4,128)S(1)} %fusion.1, f32[384,4]{0,1:T(4,128)S(1)} %get-tuple-element.28, pred[1024]{0:T(1024)(128)(4,1)S(1)} %iota_compare_fusion.4), kind=kLoop, calls=%fused_computation.7 | loop fusion | flops 7864320 | bytes 9450496 | tf_op jit(solution)/shard_map/convert_element_type | solution.py:110
  105.7 1.5 %copy.45 = bf16[1,1024,512]{1,2,0:T(8,128)(2,1)S(1)} copy(bf16[1,1024,512]{2,1,0:T(8,128)(2,1)} %get-tuple-element.24) | data formatting | bytes 2097152 | tf_op jit(solution)/shard_map/reshape | solution.py:97
  107.2 1.8 %fusion.21 = f32[4,128,384]{2,1,0:T(8,128)S(1)} fusion(bf16[1,384,4,1024]{1,3,2,0:T(8,128)(2,1)} %divide_convert_fusion, bf16[1,1024,4,128]{1,3,2,0:T(8,128)(2,1)S(1)} %bitcast.135), kind=kOutput, calls=%fused_computation.33 | convolution fusion | flops 201719808 | bytes 2883584 | tf_op jit(solution)/shard_map/rjht,rthc->rjhc/dot_general | solution.py:114
  109.0 1.9 %fusion.19 = bf16[4,128,384]{2,1,0:T(8,128)(2,1)S(1)} fusion(f32[4,128,384]{2,1,0:T(8,128)S(1)} %fusion.21, bf16[1,384,4,1024]{1,3,2,0:T(8,128)(2,1)} %divide_convert_fusion, bf16[1,1024,4,128]{1,3,2,0:T(8,128)(2,1)S(1)} %bitcast.136), kind=kOutput, calls=%fused_computation.31 | convolution fusion | flops 202113024 | bytes 3276800 | tf_op jit(solution)/shard_map/rjht,rthc->rjhc/dot_general | solution.py:114
  111.0 1.4 %fusion.15 = f32[384,512]{1,0:T(8,128)S(1)} fusion(f32[384,512]{1,0:T(8,128)S(1)} %copy-done.1, bf16[384,512]{0,1:T(8,128)(2,1)S(1)} %bitcast.138, bf16[2048,512]{1,0:T(8,128)(2,1)} %param.18, f32[512]{0:T(512)S(1)} %bitcast.146), kind=kOutput, calls=%fused_computation.27 | convolution fusion | flops 201916416 | bytes 2492416 | tf_op jit(solution)/shard_map/rje,ef->rjf/dot_general | solution.py:125
  112.4 0.8 convolution_reduce_fusion
  113.2 0.6 select_n.85
  (24 shorter events, 0.1 us)
Async XLA Ops:
  7.2 22.3 %copy-start = (bf16[1024,1024]{1,0:T(8,128)(2,1)S(1)}, bf16[1024,1024]{1,0:T(8,128)(2,1)}, u32[]{:S(2)}) copy-start(bf16[1024,1024]{1,0:T(8,128)(2,1)} %param.15) | copy-start | bytes 6291460
  13.1 26.9 %all-to-all-start = ((s32[128,1,6]{2,1,0:T(1,128)}), s32[128,1,6]{2,1,0:T(1,128)S(1)}, u32[]{:S(2)}, u32[]{:S(2)}) async-start(s32[128,1,6]{2,1,0:T(1,128)} %bitcast.2), calls=%async_computation | async-start | bytes 131072 | tf_op jit(solution)/shard_map/all_to_all | solution.py:88
  29.4 65.2 %all-gather.5.cloned.1.call-start = ((), (), s32[]{:S(2)}) async-start(), calls=%async_computation.2 | async-start | bytes 3145728 | tf_op jit(solution)/shard_map/all_gather | solution.py:93
  29.5 3.5 %copy-start.4 = (bf16[1024,1024]{1,0:T(8,128)(2,1)S(1)}, bf16[1024,1024]{1,0:T(8,128)(2,1)}, u32[]{:S(2)}) copy-start(bf16[1024,1024]{1,0:T(8,128)(2,1)} %param.16) | copy-start | bytes 6291460
  46.9 13.0 %copy-start.2 = (bf16[64,8,8,128]{3,2,1,0:T(8,128)(2,1)S(1)}, bf16[64,8,8,128]{3,2,1,0:T(8,128)(2,1)}, u32[]{:S(2)}) copy-start(bf16[64,8,8,128]{3,2,1,0:T(8,128)(2,1)} %copy.47) | copy-start | bytes 3145732
  46.9 13.0 %copy-start.5 = (bf16[1024]{0:T(1024)(128)(2,1)S(1)}, bf16[1024]{0:T(1024)(128)(2,1)}, u32[]{:S(2)}) copy-start(bf16[1024]{0:T(1024)(128)(2,1)} %param.17) | copy-start | bytes 6148
  49.5 11.5 %copy-start.6 = (u32[256]{0:T(256)S(1)}, u32[256]{0:T(256)}, u32[]{:S(2)}) copy-start(u32[256]{0:T(256)} %constant.89) | copy-start | bytes 3076
  49.5 39.3 %all-to-all-start.1 = ((bf16[128,6,512]{2,1,0:T(8,128)(2,1)}), bf16[128,6,512]{2,1,0:T(8,128)(2,1)}, u32[]{:S(2)}, u32[]{:S(2)}) async-start(bf16[128,6,512]{2,1,0:T(8,128)(2,1)} %broadcast_select_fusion), calls=%async_computation.1 | async-start | bytes 2097152 | tf_op jit(solution)/shard_map/all_to_all | solution.py:90
  109.0 2.0 %copy-start.1 = (f32[384,512]{1,0:T(8,128)S(1)}, f32[384,512]{1,0:T(8,128)}, u32[]{:S(2)}) copy-start(f32[384,512]{1,0:T(8,128)} %fusion.38) | copy-start | bytes 2359300
  109.0 3.4 %copy-start.3 = (f32[512]{0:T(512)S(1)}, f32[512]{0:T(512)}, u32[]{:S(2)}) copy-start(f32[512]{0:T(512)} %param.19) | copy-start | bytes 6148
Sparse Core Ops, SparseCore 0:
  35.4 17.9 all-gather.4
where the time goes:
time: 122 us; the launch traced here: 121 us
  starting transfers between devices  26.8 us (22%)
  local copies, waits for them, and re-layouts  22.8 us (19%)
  waiting for transfers between devices  19.8 us (16%)
  matrix products  19.2 us (16%)
  between operations  16.3 us (13%)
  other arithmetic  9.64 us (8%)
  blocking collectives  6.26 us (5%)
    all_to_all x1, starting transfers between devices, on_device(): lax.all_to_all(buckets, 'item', split_axis=0, concat_axis=0, tiled=True)  16.3 us
    all_to_all x1, waiting for transfers between devices, on_device(): lax.all_to_all(looked_up, 'item', split_axis=0, concat_axis=0, tiled=True)  16.3 us
    all_to_all x1, starting transfers between devices, on_device(): lax.all_to_all(looked_up, 'item', split_axis=0, concat_axis=0, tiled=True)  10.4 us
    gather x2, local copies, waits for them, and re-layouts, on_device(): jnp.take(table, lax.all_to_all(buckets, 'item', split_axis=0, concat_axis...  6.71 us
    dot_general x2, matrix products, on_device(): jnp.einsum('rjht,rthc->rjhc', target_weight[:, :, :, first:first + half_l...  3.77 us
    unnamed x1, blocking collectives  3.61 us
    dot_general x1, matrix products, on_device(): jnp.einsum('rtd,de->rte', history, w_event, preferred_element_type=jnp.fl...  3.46 us
    all_to_all x1, waiting for transfers between devices, on_device(): lax.all_to_all(buckets, 'item', split_axis=0, concat_axis=0, tiled=True)  3.45 us
  transfers between devices with their start and end apart: 3, of which 2 were waited for; matrix products, arithmetic and copies ran while one was open for 22% of the time, Pallas kernels for 0%

commit v1 on v0

v1 whole, which is shorter than its diff:
```python
import functools
import math

import jax
import jax.numpy as jnp
from jax import lax
from jax.experimental import pallas as pl
from jax.experimental.pallas import tpu as pltpu
from jax.sharding import PartitionSpec as P

MESH = pl.DeviceIdType.MESH
F32 = jnp.float32
BF16 = jnp.bfloat16
I32 = jnp.int32

HEAD = 128
NY, NX, NZ = 4, 4, 8
NYX = NY * NX
CAP = 6
ORDER = (4, 5, 3, 6, 2, 1, 7, 0)
GROUP = 16
NGROUP = NZ * CAP // GROUP
ROWS = 4096
E = 512
D = 1024
HALF = 512
SLOTS = 384
MASKED = -1e30
XY = tuple((dy, dx) for dy in range(NY) for dx in range(NX) if (dy, dx) != (0, 0))


def iota(shape, axis):
    return lax.broadcasted_iota(I32, shape, axis)


def dot(a, b):
    return jnp.dot(a, b, preferred_element_type=F32)


def dot_nt(a, b):
    return lax.dot_general(a, b, (((1,), (1,)), ((), ())), preferred_element_type=F32)


def kernel(
    cap_rows,
    ids_ref, len_ref, count_ref, query_ref, wout_ref,
    history, table, w_event, w_kv, w_rank,
    scores_ref, user_ref,
    hist_v, table_v, we_v, wkv_v, wr_v, states_v, kv_v,
    ids_z, got_z, turn, ids_xy, got_xy, col, pos_row, onehot,
    rows_xy, back_xy, rows_z, back_z, pool_mine, pool_other, bias,
    local_sem, z_send, z_recv, xy_send, xy_recv, rz_send, rz_recv, rxy_send, rxy_recv, pair_send, pair_recv,
):
    section = lax.axis_index("section")
    item = lax.axis_index("item")
    my_y, my_x, my_z = item // (NX * NZ), (item // NZ) % NX, item % NZ
    my_yx = item // NZ

    def load(src, dst, n):
        copy = pltpu.make_async_copy(src, dst, local_sem.at[n])
        copy.start()
        return copy

    load_hist = load(history.at[0], hist_v, 0)
    load_we = load(w_event, we_v, 1)
    load_table = load(table, table_v, 2)
    load_wkv = load(w_kv, wkv_v, 3)
    load_wr = load(w_rank, wr_v, 4)

    def z_peer(plane):
        return (section, my_yx * NZ + plane)

    def xy_index(dy, dx):
        return ((my_y + dy) % NY) * NX + (my_x + dx) % NX

    def xy_peer(yx):
        return (section, yx * NZ + my_z)

    other = (1 - section, item)
    barrier = pltpu.get_barrier_semaphore()
    for dz in range(1, NZ):
        pl.semaphore_signal(barrier, inc=1, device_id=z_peer((my_z + dz) % NZ), device_id_type=MESH)
    for dy, dx in XY:
        pl.semaphore_signal(barrier, inc=1, device_id=xy_peer(xy_index(dy, dx)), device_id_type=MESH)
    pl.semaphore_signal(barrier, inc=1, device_id=other, device_id_type=MESH)

    ids = ids_ref[...]
    owner = lax.shift_right_logical(ids, 12)
    offset = jnp.bitwise_and(ids, ROWS - 1)
    plane = jnp.bitwise_and(owner, NZ - 1)
    yx = lax.shift_right_logical(owner, 3)
    dist = jnp.bitwise_and(my_z - plane + NZ, NZ - 1)
    slot = jnp.zeros_like(dist)
    for s, dz in enumerate(ORDER):
        slot = jnp.where(dist == dz, s, slot)
    owner_hot = iota((NYX * NZ, SLOTS), 0) == owner
    before = (iota((SLOTS, SLOTS), 0) < iota((SLOTS, SLOTS), 1)).astype(F32).astype(BF16)
    earlier = dot(owner_hot.astype(F32).astype(BF16), before)
    rank = jnp.sum(jnp.where(owner_hot, earlier, 0.0), axis=0, keepdims=True).astype(I32)
    place = yx * CAP + rank
    row_of = slot * 8 + rank
    row_hot = (iota((NZ * 8, SLOTS), 0) == row_of).astype(F32).astype(BF16)
    yx_hot = iota((128, SLOTS), 0) == yx

    def spread(value):
        return dot_nt(row_hot, jnp.where(yx_hot, value.astype(F32), 0.0).astype(BF16))

    wanted = offset + 1
    message = (
        spread(jnp.bitwise_and(wanted, 63))
        + 64.0 * spread(lax.shift_right_logical(wanted, 6))
        + 8192.0 * spread(place)
    )
    ids_z[...] = message.reshape(NZ, 8, 128)
    candidate = slot * 128 + place

    pl.semaphore_wait(barrier, NZ - 1 + len(XY) + 1)

    z_ids = []
    for s, dz in enumerate(ORDER):
        if dz:
            z_ids.append(pltpu.make_async_remote_copy(
                src_ref=ids_z.at[s], dst_ref=got_z.at[s], send_sem=z_send.at[s], recv_sem=z_recv.at[s],
                device_id=z_peer((my_z - dz + NZ) % NZ), device_id_type=MESH))
            z_ids[-1].start()
        else:
            got_z[s] = ids_z[s]

    def event_rows(first):
        events = hist_v[first:first + 256, :]
        pre = dot(events, we_v[...])
        states_v[first:first + 256, :] = (events.astype(F32) + jax.nn.gelu(pre)).astype(BF16)

    load_hist.wait()
    load_we.wait()
    event_rows(0)

    for copy in z_ids:
        copy.wait_recv()
    turn[...] = jnp.zeros_like(turn)
    for s in range(NZ):
        turn[s * CAP:(s + 1) * CAP, :] = got_z[s, 0:CAP, :]
    asked = turn[...]
    turned = jnp.transpose(asked)
    for n in range(NYX):
        ids_xy[n] = jnp.broadcast_to(turned[n:n + 1, :], (8, 128))
    xy_ids = []
    for n, (dy, dx) in enumerate(XY):
        target = xy_index(dy, dx)
        xy_ids.append(pltpu.make_async_remote_copy(
            src_ref=ids_xy.at[target], dst_ref=got_xy.at[my_yx], send_sem=xy_send.at[n], recv_sem=xy_recv.at[n],
            device_id=xy_peer(target), device_id_type=MESH))
        xy_ids[-1].start()
    got_xy[my_yx] = ids_xy[my_yx]

    for g in range(NGROUP):
        for n in range(NYX):
            col[n * GROUP:(n + 1) * GROUP, :] = jnp.broadcast_to(
                asked[g * GROUP:(g + 1) * GROUP, n:n + 1], (GROUP, 128))
        pos_row[g] = jnp.transpose(col[...])

    event_rows(256)

    for copy in xy_ids:
        copy.wait_recv()
    turn[...] = jnp.zeros_like(turn)
    for n in range(NYX):
        turn[n:n + 1, :] = got_xy[n, 0:1, :]
    columns = jnp.bitwise_and(jnp.transpose(turn[...]).astype(I32), 8191)
    load_table.wait()

    xy_rows = []
    lanes = iota((1, 128), 1) + 1
    chunk = 1024
    for g in range(NGROUP):
        wants = jnp.concatenate(
            [jnp.broadcast_to(columns[g * GROUP:(g + 1) * GROUP, n:n + 1], (GROUP, 128)) for n in range(NYX)], axis=0)
        total = None
        for first in range(0, ROWS, chunk):
            for block in range(0, chunk, 128):
                onehot[:, block:block + 128] = jnp.where(
                    wants == lanes + (first + block), 1.0, 0.0).astype(BF16)
            term = dot(onehot[...], table_v[first:first + chunk, :])
            total = term if total is None else total + term
        rows_xy[g] = total.astype(BF16).reshape(NYX, GROUP, E)
        for n, (dy, dx) in enumerate(XY):
            target = xy_index(dy, dx)
            xy_rows.append(pltpu.make_async_remote_copy(
                src_ref=rows_xy.at[g, target], dst_ref=back_xy.at[g, my_yx],
                send_sem=rxy_send.at[g, n], recv_sem=rxy_recv.at[g, n],
                device_id=xy_peer(target), device_id_type=MESH))
            xy_rows[-1].start()
        back_xy[g, my_yx] = rows_xy[g, my_yx]

    load_wkv.wait()
    kv_v[section] = dot(states_v[...], wkv_v[...]).astype(BF16)
    kv_copy = pltpu.make_async_remote_copy(
        src_ref=kv_v.at[section], dst_ref=kv_v.at[section], send_sem=pair_send.at[0], recv_sem=pair_recv.at[0],
        device_id=other, device_id_type=MESH)
    kv_copy.start()

    scale = 1.0 / math.sqrt(HEAD)
    length = len_ref[0]
    heads = D // HEAD
    of_head = (iota((16, D), 1) // HEAD) == iota((16, D), 0)
    queries = jnp.where(of_head, query_ref[...].astype(F32), 0.0).astype(BF16)
    events = section * HALF + iota((1, HALF), 1)
    pool_score = jnp.where(events < length, dot_nt(queries, states_v[...]) * scale, MASKED)
    pool_max = jnp.max(pool_score, axis=-1, keepdims=True)
    pool_exp = jnp.exp(pool_score - pool_max)
    pool_sum = jnp.sum(pool_exp, axis=-1, keepdims=True)
    pooled = dot(pool_exp.astype(BF16), states_v[...])

    def by_channel(x):
        return jnp.sum(jnp.where(of_head, x, 0.0), axis=0, keepdims=True)

    pool_mine[...] = jnp.concatenate(
        [by_channel(pooled), by_channel(pool_max), by_channel(pool_sum), jnp.zeros((5, D), F32)], axis=0)
    pool_copy = pltpu.make_async_remote_copy(
        src_ref=pool_mine, dst_ref=pool_other, send_sem=pair_send.at[1], recv_sem=pair_recv.at[1],
        device_id=other, device_id_type=MESH)
    pool_copy.start()

    z_rows = []

    def forward(s):
        total = None
        for g in range(NGROUP):
            if (s + 1) * CAP <= g * GROUP or s * CAP >= (g + 1) * GROUP:
                continue
            entries = pos_row[g][0:cap_rows, :].astype(I32)
            here = jnp.bitwise_and(iota((1, NYX * GROUP), 1), GROUP - 1) + g * GROUP
            mine = (here >= s * CAP) & (here < (s + 1) * CAP)
            filled = jnp.bitwise_and(entries, 8191) > 0
            pick = (lax.shift_right_logical(entries, 13) == iota((cap_rows, NYX * GROUP), 0)) & filled & mine
            term = dot(pick.astype(F32).astype(BF16), back_xy[g].reshape(NYX * GROUP, E))
            total = term if total is None else total + term
        if ORDER[s]:
            rows_z[s] = total.astype(BF16)
            z_rows.append(pltpu.make_async_remote_copy(
                src_ref=rows_z.at[s], dst_ref=back_z.at[s], send_sem=rz_send.at[s], recv_sem=rz_recv.at[s],
                device_id=z_peer((my_z + ORDER[s]) % NZ), device_id_type=MESH))
            z_rows[-1].start()
        else:
            back_z[s] = total.astype(BF16)

    for g in range(NGROUP):
        for copy in xy_rows[g * len(XY):(g + 1) * len(XY)]:
            copy.wait_recv()
        for s in range(NZ):
            if g * GROUP < (s + 1) * CAP <= (g + 1) * GROUP:
                forward(s)

    pool_copy.wait_recv()
    mine, theirs = pool_mine[...], pool_other[...]
    first = jnp.where(section == 0, mine, theirs)
    second = jnp.where(section == 0, theirs, mine)
    joint = jnp.maximum(first[1:2], second[1:2])
    first_scale, second_scale = jnp.exp(first[1:2] - joint), jnp.exp(second[1:2] - joint)
    state = (first[0:1] * first_scale + second[0:1] * second_scale) / (
        first[2:3] * first_scale + second[2:3] * second_scale)
    state = state.astype(BF16)
    user_ref[...] = state
    load_wr.wait()
    user_term = dot(jnp.broadcast_to(state, (16, D)), wr_v[2 * E:, :])[0:1]
    kv_copy.wait_recv()
    bias[...] = jnp.where(iota((8, 2 * HALF), 1) < length, 0.0, MASKED)

    def attend(turn_number, so_far):
        s = (turn_number + NZ - 1) % NZ

        @pl.when(s != NZ - 1)
        def _():
            pltpu.make_async_remote_copy(
                src_ref=rows_z.at[s], dst_ref=back_z.at[s], send_sem=rz_send.at[s], recv_sem=rz_recv.at[s],
                device_id=other, device_id_type=MESH).wait_recv()

        rows = back_z[s]
        parts = []
        for h in range(E // HEAD):
            c = h * HEAD
            keys = kv_v[:, :, c:c + HEAD].reshape(2 * HALF, HEAD)
            score = dot_nt(rows[:, c:c + HEAD], keys) * scale + bias[0:1]
            top = jnp.max(score, axis=-1, keepdims=True)
            expo = jnp.exp(score - top)
            inverse = 1.0 / jnp.sum(expo, axis=-1, keepdims=True)
            weight = (expo * inverse).astype(BF16)
            halves = [
                dot(weight[:, k * HALF:(k + 1) * HALF], kv_v[k, :, E + c:E + c + HEAD]).astype(BF16).astype(F32)
                for k in range(2)]
            parts.append((halves[0] + halves[1]).astype(BF16))
        attended = jnp.concatenate(parts, axis=-1)
        hidden = dot(rows, wr_v[0:E, :]) + dot(attended, wr_v[E:2 * E, :]) + user_term
        score = jnp.sum(jnp.maximum(hidden, 0.0) * wout_ref[...], axis=-1, keepdims=True)
        mine = (iota((cap_rows, SLOTS), 0) + s * 128) == candidate
        return so_far + jnp.sum(jnp.where(mine, score, 0.0), axis=0, keepdims=True)

    found = lax.fori_loop(0, NZ, attend, jnp.zeros((1, SLOTS), F32))
    live = section * SLOTS + iota((1, SLOTS), 1) < count_ref[0]
    scores_ref[...] = jnp.where(live, found, 0.0)

    for copy in z_ids + xy_ids + xy_rows + z_rows + [kv_copy, pool_copy]:
        copy.wait_send()


def fetch_and_rank(cap_rows, collective_id, hist_len, cand_ids, cand_count, pool_query, w_out, history, table,
                   w_event, w_kv, w_rank):
    vmem = pl.BlockSpec(memory_space=pltpu.VMEM)
    smem = pl.BlockSpec(memory_space=pltpu.SMEM)
    anywhere = pl.BlockSpec(memory_space=pl.ANY)
    dma = pltpu.SemaphoreType.DMA
    scratch = [
        pltpu.VMEM((HALF, D), BF16), pltpu.VMEM((ROWS, E), BF16), pltpu.VMEM((D, D), BF16),
        pltpu.VMEM((D, 2 * E), BF16), pltpu.VMEM((2 * E + D, E), BF16), pltpu.VMEM((HALF, D), BF16),
        pltpu.VMEM((2, HALF, 2 * E), BF16),
        pltpu.VMEM((NZ, 8, 128), F32), pltpu.VMEM((NZ, 8, 128), F32), pltpu.VMEM((128, 128), F32),
        pltpu.VMEM((NYX, 8, 128), F32), pltpu.VMEM((NYX, 8, 128), F32),
        pltpu.VMEM((NYX * GROUP, 128), F32), pltpu.VMEM((NGROUP, 128, NYX * GROUP), F32),
        pltpu.VMEM((NYX * GROUP, 1024), BF16),
        pltpu.VMEM((NGROUP, NYX, GROUP, E), BF16), pltpu.VMEM((NGROUP, NYX, GROUP, E), BF16),
        pltpu.VMEM((NZ, cap_rows, E), BF16), pltpu.VMEM((NZ, cap_rows, E), BF16),
        pltpu.VMEM((8, D), F32), pltpu.VMEM((8, D), F32), pltpu.VMEM((8, 2 * HALF), F32),
        dma((5,)), dma((NZ,)), dma((NZ,)), dma((len(XY),)), dma((len(XY),)), dma((NZ,)), dma((NZ,)),
        dma((NGROUP, len(XY))), dma((NGROUP, len(XY))), dma((2,)), dma((2,)),
    ]
    return pl.pallas_call(
        functools.partial(kernel, cap_rows),
        out_shape=(jax.ShapeDtypeStruct((1, SLOTS), F32), jax.ShapeDtypeStruct((1, D), BF16)),
        in_specs=[vmem, smem, smem, vmem, vmem] + [anywhere] * 5,
        out_specs=(vmem, vmem),
        scratch_shapes=scratch,
        compiler_params=pltpu.CompilerParams(
            collective_id=collective_id, has_side_effects=True, vmem_limit_bytes=48 * 1024 * 1024),
        name="fetch_and_rank",
    )(cand_ids, hist_len, cand_count, pool_query.reshape(1, D), w_out.reshape(1, E), history, table, w_event, w_kv,
      w_rank)


def on_device(
    history, hist_len, cand_ids, cand_count, table, w_event, w_kv, pool_query, w_rank, w_out
):
    return fetch_and_rank(
        NYX * CAP, 0, hist_len, cand_ids, cand_count, pool_query, w_out, history, table, w_event, w_kv, w_rank)


def solution(mesh):
    placed = (
        P("item", "section", None),
        P("item"),
        P("item", "section"),
        P("item"),
        P("item", None),
        P(),
        P(),
        P(),
        P(),
        P(),
    )
    return jax.shard_map(
        on_device,
        mesh=mesh,
        in_specs=placed,
        out_specs=(P("item", "section"), P("item", None)),
        check_vma=False,
    )
```

time: 122 us -> 65.1 us (0.53)
  the two profiles are of different devices: /device:TPU:1 before, /device:TPU:64 now
where the time goes in v1:
time: 65.1 us; the launch traced here: 64.9 us
  Pallas kernels  55.3 us (85%)
  local copies, waits for them, and re-layouts  7.61 us (12%)
  between operations  1.94 us (3%)
    pallas_call x1, Pallas kernels, fetch_and_rank(): pl.pallas_call(functools.partial(kernel, cap_rows), out_shape=(jax.ShapeD...  55.3 us
    unnamed x12, local copies, waits for them, and re-layouts  6.92 us

profile of v1, /device:TPU:64, one launch (start us, length us, event | category | flops | bytes accessed | tf_op | source)
XLA Modules:
  0.0 64.9 jit_solution(2094230598581351551)
XLA Ops:
  1.9 0.7 %reshape.10.query_ref = bf16[1,1024]{1,0:T(2,128)(2,1)S(1)} reshape(bf16[1024]{0:T(1024)(128)(2,1)} %param.17) | data formatting | bytes 4096 | tf_op jit(solution)/shard_map/reshape | solution.py:335
  2.6 0.0 copy-start
  2.6 1.6 %copy-done = bf16[1024,1024]{1,0:T(8,128)(2,1)S(1)} copy-done((bf16[1024,1024]{1,0:T(8,128)(2,1)S(1)}, bf16[1024,1024]{1,0:T(8,128)(2,1)}, u32[]{:S(2)}) %copy-start) | copy-done | bytes 2097176
  4.2 0.0 copy-start.1
  4.2 1.6 %copy-done.1 = bf16[1024,1024]{1,0:T(8,128)(2,1)S(1)} copy-done((bf16[1024,1024]{1,0:T(8,128)(2,1)S(1)}, bf16[1024,1024]{1,0:T(8,128)(2,1)}, u32[]{:S(2)}) %copy-start.1) | copy-done | bytes 2097176
  5.8 0.0 copy-start.2
  5.8 1.2 %copy-done.2 = bf16[1,512,1024]{2,1,0:T(8,128)(2,1)S(1)} copy-done((bf16[1,512,1024]{2,1,0:T(8,128)(2,1)S(1)}, bf16[1,512,1024]{2,1,0:T(8,128)(2,1)}, u32[]{:S(2)}) %copy-start.2) | copy-done | bytes 1048600
  7.0 0.0 copy-start.3
  7.0 0.7 %copy-done.3 = f32[512]{0:T(512)S(1)} copy-done((f32[512]{0:T(512)S(1)}, f32[512]{0:T(512)}, u32[]{:S(2)}) %copy-start.3) | copy-done | bytes 2072
  7.7 0.0 copy-start.4
  7.7 0.7 %copy-done.4 = s32[1,384]{1,0:T(1,128)S(1)} copy-done((s32[1,384]{1,0:T(1,128)S(1)}, s32[1,384]{1,0:T(1,128)}, u32[]{:S(2)}) %copy-start.4) | copy-done | bytes 1560
  8.4 55.3 %fetch_and_rank.1 = (f32[1,384]{1,0:T(1,128)S(1)}, bf16[1,1024]{1,0:T(2,128)(2,1)S(1)}) custom-call(s32[1,384]{1,0:T(1,128)S(1)} %copy-done.4, s32[1]{0:T(128)S(6)} %copy.14.len_ref, s32[1]{0:T(128)S(6)} %copy.15.count_ref, bf16[1,1024]{1,0:T(2,128)(2,1)S(1)} %reshape.10.query_ref, f32[1,512]{1,0:T(1,128)S(1)} %bitcast.1, ...), custom_call_target="tpu_custom_call" | custom-call | tf_op jit(solution)/shard_map/fetch_and_rank/pallas_call | solution.py:326
  63.7 0.6 copy.16
  64.3 0.6 copy.17
Async XLA Ops:
  2.6 1.6 %copy-start = (bf16[1024,1024]{1,0:T(8,128)(2,1)S(1)}, bf16[1024,1024]{1,0:T(8,128)(2,1)}, u32[]{:S(2)}) copy-start(bf16[1024,1024]{1,0:T(8,128)(2,1)} %w_event.1) | copy-start | bytes 6291460
  4.2 1.6 %copy-start.1 = (bf16[1024,1024]{1,0:T(8,128)(2,1)S(1)}, bf16[1024,1024]{1,0:T(8,128)(2,1)}, u32[]{:S(2)}) copy-start(bf16[1024,1024]{1,0:T(8,128)(2,1)} %w_kv.1) | copy-start | bytes 6291460
  5.8 1.2 %copy-start.2 = (bf16[1,512,1024]{2,1,0:T(8,128)(2,1)S(1)}, bf16[1,512,1024]{2,1,0:T(8,128)(2,1)}, u32[]{:S(2)}) copy-start(bf16[1,512,1024]{2,1,0:T(8,128)(2,1)} %history.1) | copy-start | bytes 3145732
  7.0 0.7 %copy-start.3 = (f32[512]{0:T(512)S(1)}, f32[512]{0:T(512)}, u32[]{:S(2)}) copy-start(f32[512]{0:T(512)} %param.19) | copy-start | bytes 6148
  7.7 0.7 %copy-start.4 = (s32[1,384]{1,0:T(1,128)S(1)}, s32[1,384]{1,0:T(1,128)}, u32[]{:S(2)}) copy-start(s32[1,384]{1,0:T(1,128)} %ids_ref.1) | copy-start | bytes 4612

commit v2 on v1

--- a/solution.py
+++ b/solution.py
@@ -18,6 +18,7 @@
 NYX = NY * NX
 CAP = 6
 ORDER = (4, 5, 3, 6, 2, 1, 7, 0)
+ROOM = 64
 GROUP = 16
 NGROUP = NZ * CAP // GROUP
 ROWS = 4096
@@ -45,10 +46,10 @@
     cap_rows,
     ids_ref, len_ref, count_ref, query_ref, wout_ref,
     history, table, w_event, w_kv, w_rank,
-    scores_ref, user_ref,
+    scores_ref, user_ref, over_ref,
     hist_v, table_v, we_v, wkv_v, wr_v, states_v, kv_v,
     ids_z, got_z, turn, ids_xy, got_xy, col, pos_row, onehot,
-    rows_xy, back_xy, rows_z, back_z, pool_mine, pool_other, bias,
+    rows_xy, back_xy, rows_z, back_z, pool_mine, pool_other, keys_v, values_v,
     local_sem, z_send, z_recv, xy_send, xy_recv, rz_send, rz_recv, rxy_send, rxy_recv, pair_send, pair_recv,
 ):
     section = lax.axis_index("section")
@@ -95,9 +96,16 @@
         slot = jnp.where(dist == dz, s, slot)
     owner_hot = iota((NYX * NZ, SLOTS), 0) == owner
     before = (iota((SLOTS, SLOTS), 0) < iota((SLOTS, SLOTS), 1)).astype(F32).astype(BF16)
-    earlier = dot(owner_hot.astype(F32).astype(BF16), before)
-    rank = jnp.sum(jnp.where(owner_hot, earlier, 0.0), axis=0, keepdims=True).astype(I32)
-    place = yx * CAP + rank
+    slot_hot = iota((16, SLOTS), 0) == slot
+    hot = jnp.concatenate([owner_hot.astype(F32), slot_hot.astype(F32)], axis=0).astype(BF16)
+    earlier = dot(hot, before)
+    owners = NYX * NZ
+    rank = jnp.sum(jnp.where(owner_hot, earlier[0:owners], 0.0), axis=0, keepdims=True).astype(I32)
+    if cap_rows < NYX * CAP:
+        place = jnp.sum(jnp.where(slot_hot, earlier[owners:], 0.0), axis=0, keepdims=True).astype(I32)
+    else:
+        place = yx * CAP + rank
+    over = jnp.max(jnp.where(place < cap_rows, 0.0, 1.0), axis=1, keepdims=True)
     row_of = slot * 8 + rank
     row_hot = (iota((NZ * 8, SLOTS), 0) == row_of).astype(F32).astype(BF16)
     yx_hot = iota((128, SLOTS), 0) == yx
@@ -111,8 +119,9 @@
         + 64.0 * spread(lax.shift_right_logical(wanted, 6))
         + 8192.0 * spread(place)
     )
+    message = message + jnp.where(jnp.bitwise_and(iota((NZ * 8, 128), 0), 7) == CAP, over, 0.0)
     ids_z[...] = message.reshape(NZ, 8, 128)
-    candidate = slot * 128 + place
+    candidate = slot * cap_rows + place
 
     pl.semaphore_wait(barrier, NZ - 1 + len(XY) + 1)
 
@@ -126,15 +135,6 @@
         else:
             got_z[s] = ids_z[s]
 
-    def event_rows(first):
-        events = hist_v[first:first + 256, :]
-        pre = dot(events, we_v[...])
-        states_v[first:first + 256, :] = (events.astype(F32) + jax.nn.gelu(pre)).astype(BF16)
-
-    load_hist.wait()
-    load_we.wait()
-    event_rows(0)
-
     for copy in z_ids:
         copy.wait_recv()
     turn[...] = jnp.zeros_like(turn)
@@ -142,8 +142,9 @@
         turn[s * CAP:(s + 1) * CAP, :] = got_z[s, 0:CAP, :]
     asked = turn[...]
     turned = jnp.transpose(asked)
+    over = jnp.max(got_z[:, CAP, :], axis=0, keepdims=True)
     for n in range(NYX):
-        ids_xy[n] = jnp.broadcast_to(turned[n:n + 1, :], (8, 128))
+        ids_xy[n] = jnp.where(iota((8, 128), 0) == 0, turned[n:n + 1, :], over)
     xy_ids = []
     for n, (dy, dx) in enumerate(XY):
         target = xy_index(dy, dx)
@@ -159,13 +160,12 @@
                 asked[g * GROUP:(g + 1) * GROUP, n:n + 1], (GROUP, 128))
         pos_row[g] = jnp.transpose(col[...])
 
-    event_rows(256)
-
     for copy in xy_ids:
         copy.wait_recv()
     turn[...] = jnp.zeros_like(turn)
     for n in range(NYX):
         turn[n:n + 1, :] = got_xy[n, 0:1, :]
+    over = jnp.max(got_xy[:, 1, :], axis=0, keepdims=True)
     columns = jnp.bitwise_and(jnp.transpose(turn[...]).astype(I32), 8191)
     load_table.wait()
 
@@ -192,36 +192,19 @@
             xy_rows[-1].start()
         back_xy[g, my_yx] = rows_xy[g, my_yx]
 
-    load_wkv.wait()
-    kv_v[section] = dot(states_v[...], wkv_v[...]).astype(BF16)
-    kv_copy = pltpu.make_async_remote_copy(
-        src_ref=kv_v.at[section], dst_ref=kv_v.at[section], send_sem=pair_send.at[0], recv_sem=pair_recv.at[0],
-        device_id=other, device_id_type=MESH)
-    kv_copy.start()
-
-    scale = 1.0 / math.sqrt(HEAD)
-    length = len_ref[0]
-    heads = D // HEAD
-    of_head = (iota((16, D), 1) // HEAD) == iota((16, D), 0)
-    queries = jnp.where(of_head, query_ref[...].astype(F32), 0.0).astype(BF16)
-    events = section * HALF + iota((1, HALF), 1)
-    pool_score = jnp.where(events < length, dot_nt(queries, states_v[...]) * scale, MASKED)
-    pool_max = jnp.max(pool_score, axis=-1, keepdims=True)
-    pool_exp = jnp.exp(pool_score - pool_max)
-    pool_sum = jnp.sum(pool_exp, axis=-1, keepdims=True)
-    pooled = dot(pool_exp.astype(BF16), states_v[...])
-
-    def by_channel(x):
-        return jnp.sum(jnp.where(of_head, x, 0.0), axis=0, keepdims=True)
-
-    pool_mine[...] = jnp.concatenate(
-        [by_channel(pooled), by_channel(pool_max), by_channel(pool_sum), jnp.zeros((5, D), F32)], axis=0)
-    pool_copy = pltpu.make_async_remote_copy(
-        src_ref=pool_mine, dst_ref=pool_other, send_sem=pair_send.at[1], recv_sem=pair_recv.at[1],
-        device_id=other, device_id_type=MESH)
-    pool_copy.start()
+    load_hist.wait()
+    load_we.wait()
+    for first in range(0, HALF, 256):
+        events = hist_v[first:first + 256, :]
+        pre = dot(events, we_v[...])
+        states_v[first:first + 256, :] = (events.astype(F32) + jax.nn.gelu(pre)).astype(BF16)
 
     z_rows = []
+
+    def z_copy(s, src, dst, plane):
+        return pltpu.make_async_remote_copy(
+            src_ref=src, dst_ref=dst, send_sem=rz_send.at[s], recv_sem=rz_recv.at[s],
+            device_id=z_peer(plane), device_id_type=MESH)
 
     def forward(s):
         total = None
@@ -237,19 +220,51 @@
             total = term if total is None else total + term
         if ORDER[s]:
             rows_z[s] = total.astype(BF16)
-            z_rows.append(pltpu.make_async_remote_copy(
-                src_ref=rows_z.at[s], dst_ref=back_z.at[s], send_sem=rz_send.at[s], recv_sem=rz_recv.at[s],
-                device_id=z_peer((my_z + ORDER[s]) % NZ), device_id_type=MESH))
+            z_rows.append(z_copy(s, rows_z.at[s], back_z.at[s], (my_z + ORDER[s]) % NZ))
             z_rows[-1].start()
         else:
             back_z[s] = total.astype(BF16)
 
-    for g in range(NGROUP):
+    def forward_group(g):
         for copy in xy_rows[g * len(XY):(g + 1) * len(XY)]:
             copy.wait_recv()
         for s in range(NZ):
             if g * GROUP < (s + 1) * CAP <= (g + 1) * GROUP:
                 forward(s)
+
+    forward_group(0)
+
+    load_wkv.wait()
+    kv_v[section] = dot(states_v[...], wkv_v[...]).astype(BF16)
+    kv_copy = pltpu.make_async_remote_copy(
+        src_ref=kv_v.at[section], dst_ref=kv_v.at[section], send_sem=pair_send.at[0], recv_sem=pair_recv.at[0],
+        device_id=other, device_id_type=MESH)
+    kv_copy.start()
+
+    scale = 1.0 / math.sqrt(HEAD)
+    length = len_ref[0]
+    of_head = (iota((16, D), 1) // HEAD) == iota((16, D), 0)
+    queries = jnp.where(of_head, query_ref[...].astype(F32).reshape(1, D), 0.0).astype(BF16)
+    events = section * HALF + iota((1, HALF), 1)
+    pool_score = jnp.where(events < length, dot_nt(queries, states_v[...]) * scale, MASKED)
+    pool_max = jnp.max(pool_score, axis=-1, keepdims=True)
+    pool_exp = jnp.exp(pool_score - pool_max)
+    pool_sum = jnp.sum(pool_exp, axis=-1, keepdims=True)
+    pooled = dot(pool_exp.astype(BF16), states_v[...])
+
+    def by_channel(x):
+        return jnp.sum(jnp.where(of_head, x, 0.0), axis=0, keepdims=True)
+
+    pool_mine[...] = jnp.concatenate(
+        [by_channel(pooled), by_channel(pool_max), by_channel(pool_sum)]
+        + [jnp.concatenate([over] * (D // 128), axis=1)] * 5, axis=0)
+    pool_copy = pltpu.make_async_remote_copy(
+        src_ref=pool_mine, dst_ref=pool_other, send_sem=pair_send.at[1], recv_sem=pair_recv.at[1],
+        device_id=other, device_id_type=MESH)
+    pool_copy.start()
+
+    forward_group(1)
+    forward_group(2)
 
     pool_copy.wait_recv()
     mine, theirs = pool_mine[...], pool_other[...]
@@ -261,41 +276,51 @@
         first[2:3] * first_scale + second[2:3] * second_scale)
     state = state.astype(BF16)
     user_ref[...] = state
+    over_ref[...] = jnp.maximum(mine[3:4, 0:128], theirs[3:4, 0:128])
     load_wr.wait()
     user_term = dot(jnp.broadcast_to(state, (16, D)), wr_v[2 * E:, :])[0:1]
     kv_copy.wait_recv()
-    bias[...] = jnp.where(iota((8, 2 * HALF), 1) < length, 0.0, MASKED)
-
-    def attend(turn_number, so_far):
-        s = (turn_number + NZ - 1) % NZ
-
-        @pl.when(s != NZ - 1)
-        def _():
-            pltpu.make_async_remote_copy(
-                src_ref=rows_z.at[s], dst_ref=back_z.at[s], send_sem=rz_send.at[s], recv_sem=rz_recv.at[s],
-                device_id=other, device_id_type=MESH).wait_recv()
-
-        rows = back_z[s]
+    for k in range(2):
+        keys_v[:, k * HALF:(k + 1) * HALF] = jnp.transpose(kv_v[k, :, 0:E])
+        for h in range(E // HEAD):
+            values_v[h, k * HALF:(k + 1) * HALF, 0:HEAD] = kv_v[k, :, E + h * HEAD:E + (h + 1) * HEAD]
+            values_v[h, k * HALF:(k + 1) * HALF, HEAD:] = jnp.ones((HALF, HEAD), BF16)
+    bias = jnp.where(iota((1, 2 * HALF), 1) < length, 0.0, MASKED)
+
+    pair = 2 * cap_rows
+
+    def attend(step, so_far):
+        for s in (2 * step, 2 * step + 1):
+            @pl.when(s != NZ - 1)
+            def _():
+                z_copy(s, rows_z.at[s], back_z.at[s], my_z).wait_recv()
+
+        rows = back_z[pl.ds(2 * step, 2)].reshape(pair, E)
+
+        def scores(h):
+            return dot(rows[:, h * HEAD:(h + 1) * HEAD], keys_v[h * HEAD:(h + 1) * HEAD, :])
+
+        heads_total = E // HEAD
+        ready = scores(0)
         parts = []
-        for h in range(E // HEAD):
-            c = h * HEAD
-            keys = kv_v[:, :, c:c + HEAD].reshape(2 * HALF, HEAD)
-            score = dot_nt(rows[:, c:c + HEAD], keys) * scale + bias[0:1]
-            top = jnp.max(score, axis=-1, keepdims=True)
-            expo = jnp.exp(score - top)
-            inverse = 1.0 / jnp.sum(expo, axis=-1, keepdims=True)
-            weight = (expo * inverse).astype(BF16)
-            halves = [
-                dot(weight[:, k * HALF:(k + 1) * HALF], kv_v[k, :, E + c:E + c + HEAD]).astype(BF16).astype(F32)
-                for k in range(2)]
-            parts.append((halves[0] + halves[1]).astype(BF16))
+        for h in range(heads_total):
+            score = ready * (scale * math.log2(math.e)) + bias
+            if h + 1 < heads_total:
+                ready = scores(h + 1)
+            expo = jnp.exp2(score - jnp.max(score, axis=-1, keepdims=True)).astype(BF16)
+            early = dot(expo[:, 0:HALF], values_v[h, 0:HALF, :])
+            late = dot(expo[:, HALF:], values_v[h, HALF:, :])
+            inverse = 1.0 / (early[:, HEAD:] + late[:, HEAD:])
+            early = (early[:, 0:HEAD] * inverse).astype(BF16).astype(F32)
+            late = (late[:, 0:HEAD] * inverse).astype(BF16).astype(F32)
+            parts.append((early + late).astype(BF16))
         attended = jnp.concatenate(parts, axis=-1)
         hidden = dot(rows, wr_v[0:E, :]) + dot(attended, wr_v[E:2 * E, :]) + user_term
         score = jnp.sum(jnp.maximum(hidden, 0.0) * wout_ref[...], axis=-1, keepdims=True)
-        mine = (iota((cap_rows, SLOTS), 0) + s * 128) == candidate
+        mine = (iota((pair, SLOTS), 0) + step * pair) == candidate
         return so_far + jnp.sum(jnp.where(mine, score, 0.0), axis=0, keepdims=True)
 
-    found = lax.fori_loop(0, NZ, attend, jnp.zeros((1, SLOTS), F32))
+    found = lax.fori_loop(0, NZ // 2, attend, jnp.zeros((1, SLOTS), F32))
     live = section * SLOTS + iota((1, SLOTS), 1) < count_ref[0]
     scores_ref[...] = jnp.where(live, found, 0.0)
 
@@ -319,28 +344,34 @@
         pltpu.VMEM((NYX * GROUP, 1024), BF16),
         pltpu.VMEM((NGROUP, NYX, GROUP, E), BF16), pltpu.VMEM((NGROUP, NYX, GROUP, E), BF16),
         pltpu.VMEM((NZ, cap_rows, E), BF16), pltpu.VMEM((NZ, cap_rows, E), BF16),
-        pltpu.VMEM((8, D), F32), pltpu.VMEM((8, D), F32), pltpu.VMEM((8, 2 * HALF), F32),
+        pltpu.VMEM((8, D), F32), pltpu.VMEM((8, D), F32),
+        pltpu.VMEM((E, 2 * HALF), BF16), pltpu.VMEM((E // HEAD, 2 * HALF, 2 * HEAD), BF16),
         dma((5,)), dma((NZ,)), dma((NZ,)), dma((len(XY),)), dma((len(XY),)), dma((NZ,)), dma((NZ,)),
         dma((NGROUP, len(XY))), dma((NGROUP, len(XY))), dma((2,)), dma((2,)),
     ]
     return pl.pallas_call(
         functools.partial(kernel, cap_rows),
-        out_shape=(jax.ShapeDtypeStruct((1, SLOTS), F32), jax.ShapeDtypeStruct((1, D), BF16)),
+        out_shape=(
+            jax.ShapeDtypeStruct((1, SLOTS), F32), jax.ShapeDtypeStruct((1, D), BF16),
+            jax.ShapeDtypeStruct((1, 128), F32)),
         in_specs=[vmem, smem, smem, vmem, vmem] + [anywhere] * 5,
-        out_specs=(vmem, vmem),
+        out_specs=(vmem, vmem, vmem),
         scratch_shapes=scratch,
         compiler_params=pltpu.CompilerParams(
-            collective_id=collective_id, has_side_effects=True, vmem_limit_bytes=48 * 1024 * 1024),
+            collective_id=collective_id, has_side_effects=True, vmem_limit_bytes=60 * 1024 * 1024),
         name="fetch_and_rank",
-    )(cand_ids, hist_len, cand_count, pool_query.reshape(1, D), w_out.reshape(1, E), history, table, w_event, w_kv,
+    )(cand_ids, hist_len, cand_count, pool_query, w_out.reshape(1, E), history, table, w_event, w_kv,
       w_rank)
 
 
 def on_device(
     history, hist_len, cand_ids, cand_count, table, w_event, w_kv, pool_query, w_rank, w_out
 ):
-    return fetch_and_rank(
-        NYX * CAP, 0, hist_len, cand_ids, cand_count, pool_query, w_out, history, table, w_event, w_kv, w_rank)
+    operands = (hist_len, cand_ids, cand_count, pool_query, w_out, history, table, w_event, w_kv, w_rank)
+    scores, user_state, over = fetch_and_rank(ROOM, 0, *operands)
+    scores = lax.cond(
+        over[0, 0] > 0.0, lambda: fetch_and_rank(NYX * CAP, 1, *operands)[0], lambda: scores)
+    return scores, user_state
 
 
 def solution(mesh):

time: 65.1 us -> 48.1 us (0.74)
  the two profiles are of different devices: /device:TPU:64 before, /device:TPU:8 now
where the time goes in v2:
time: 48.1 us; the launch traced here: 48 us
  Pallas kernels  44 us (91%)
  between operations  2.66 us (6%)
  local copies, waits for them, and re-layouts  1.18 us (2%)
    pallas_call x1, Pallas kernels, fetch_and_rank(): pl.pallas_call(functools.partial(kernel, cap_rows), out_shape=(jax.ShapeD...  44 us
    unnamed x14, local copies, waits for them, and re-layouts  1.18 us

profile of v2, /device:TPU:8, one launch (start us, length us, event | category | flops | bytes accessed | tf_op | source)
XLA Modules:
  0.0 48.0 jit_solution(12137855995672879820)
XLA Ops:
  1.9 0.0 copy-start
  1.9 0.0 copy-start.1
  1.9 0.0 copy-start.2
  2.0 0.0 copy-start.3
  2.0 0.0 copy-start.4
  2.0 44.0 %fetch_and_rank.3 = (f32[1,384]{1,0:T(1,128)S(1)}, bf16[1,1024]{1,0:T(2,128)(2,1)}, f32[1,128]{1,0:T(1,128)}) custom-call(s32[1,384]{1,0:T(1,128)} %ids_ref.1, s32[1]{0:T(128)S(6)} %copy.16.len_ref, s32[1]{0:T(128)S(6)} %copy.17.count_ref, bf16[1024]{0:T(1024)(128)(2,1)} %query_ref.1, f32[1,512]{1,0:T(1,128)} %bitcast.4, bf16[1,512,1024]{2,1,0:T(8,128)(2,1)} %history.1, ...), custom_call_target="tpu_custom_call" | custom-call | tf_op jit(solution)/shard_map/fetch_and_rank/pallas_call | solution.py:352
  46.6 0.0 copy-done
  46.6 0.0 copy-done.1
  46.6 0.0 copy-done.2
  46.6 0.0 copy-done.3
  46.6 0.0 copy-done.4
  46.6 0.0 copy-start.5
  46.7 0.2 conditional.1
  46.9 0.6 %copy.18 = f32[1,384]{1,0:T(1,128)} copy(f32[1,384]{1,0:T(1,128)S(1)} %get-tuple-element.47) | data formatting | bytes 3072
  47.4 0.0 copy-done.5
  47.4 0.6 %copy.19 = bf16[1,1024]{1,0:T(2,128)(2,1)} copy(bf16[1,1024]{1,0:T(2,128)(2,1)S(1)} %copy-done.5) | data formatting | bytes 4096
Async XLA Ops:
  1.9 44.7 %copy-start = (bf16[1024,1024]{1,0:T(8,128)(2,1)S(1)}, bf16[1024,1024]{1,0:T(8,128)(2,1)}, u32[]{:S(2)}) copy-start(bf16[1024,1024]{1,0:T(8,128)(2,1)} %w_event.1) | copy-start | bytes 6291460
  1.9 44.7 %copy-start.1 = (bf16[1,512,1024]{2,1,0:T(8,128)(2,1)S(1)}, bf16[1,512,1024]{2,1,0:T(8,128)(2,1)}, u32[]{:S(2)}) copy-start(bf16[1,512,1024]{2,1,0:T(8,128)(2,1)} %history.1) | copy-start | bytes 3145732
  1.9 44.7 %copy-start.2 = (bf16[1024]{0:T(1024)(128)(2,1)S(1)}, bf16[1024]{0:T(1024)(128)(2,1)}, u32[]{:S(2)}) copy-start(bf16[1024]{0:T(1024)(128)(2,1)} %query_ref.1) | copy-start | bytes 6148
  2.0 44.7 %copy-start.3 = (f32[512]{0:T(512)S(1)}, f32[512]{0:T(512)}, u32[]{:S(2)}) copy-start(f32[512]{0:T(512)} %param.21) | copy-start | bytes 6148
  2.0 44.7 %copy-start.4 = (s32[1,384]{1,0:T(1,128)S(1)}, s32[1,384]{1,0:T(1,128)}, u32[]{:S(2)}) copy-start(s32[1,384]{1,0:T(1,128)} %ids_ref.1) | copy-start | bytes 4612
  46.6 0.8 %copy-start.5 = (bf16[1,1024]{1,0:T(2,128)(2,1)S(1)}, bf16[1,1024]{1,0:T(2,128)(2,1)}, u32[]{:S(2)}) copy-start(bf16[1,1024]{1,0:T(2,128)(2,1)} %get-tuple-element.46) | copy-start | bytes 6148

commit v3 on v2

--- a/solution.py
+++ b/solution.py
@@ -18,7 +18,7 @@
 NYX = NY * NX
 CAP = 6
 ORDER = (4, 5, 3, 6, 2, 1, 7, 0)
-ROOM = 64
+ROOM = 56
 GROUP = 16
 NGROUP = NZ * CAP // GROUP
 ROWS = 4096
@@ -44,10 +44,10 @@
 
 def kernel(
     cap_rows,
-    ids_ref, len_ref, count_ref, query_ref, wout_ref,
+    len_ref, count_ref, cand_ids, pool_query, w_out,
     history, table, w_event, w_kv, w_rank,
     scores_ref, user_ref, over_ref,
-    hist_v, table_v, we_v, wkv_v, wr_v, states_v, kv_v,
+    ids_v, query_v, wout_v, user_v, over_v, hist_v, table_v, we_v, wkv_v, wr_v, states_v, kv_v,
     ids_z, got_z, turn, ids_xy, got_xy, col, pos_row, onehot,
     rows_xy, back_xy, rows_z, back_z, pool_mine, pool_other, keys_v, values_v,
     local_sem, z_send, z_recv, xy_send, xy_recv, rz_send, rz_recv, rxy_send, rxy_recv, pair_send, pair_recv,
@@ -62,11 +62,11 @@
         copy.start()
         return copy
 
-    load_hist = load(history.at[0], hist_v, 0)
-    load_we = load(w_event, we_v, 1)
-    load_table = load(table, table_v, 2)
-    load_wkv = load(w_kv, wkv_v, 3)
-    load_wr = load(w_rank, wr_v, 4)
+    load_ids = load(cand_ids, ids_v, 5)
+
+    def drain(block, sem):
+        pltpu.make_async_copy(block, block, sem).wait()
+
 
     def z_peer(plane):
         return (section, my_yx * NZ + plane)
@@ -85,7 +85,16 @@
         pl.semaphore_signal(barrier, inc=1, device_id=xy_peer(xy_index(dy, dx)), device_id_type=MESH)
     pl.semaphore_signal(barrier, inc=1, device_id=other, device_id_type=MESH)
 
-    ids = ids_ref[...]
+    load_hist = load(history.at[0], hist_v, 0)
+    load_we = load(w_event, we_v, 1)
+    load_table = load(table, table_v, 2)
+    load_wkv = load(w_kv, wkv_v, 3)
+    load_wr = load(w_rank, wr_v, 4)
+    load_query = load(pool_query, query_v, 6)
+    load_wout = load(w_out, wout_v, 7)
+
+    load_ids.wait()
+    ids = ids_v[...]
     owner = lax.shift_right_logical(ids, 12)
     offset = jnp.bitwise_and(ids, ROWS - 1)
     plane = jnp.bitwise_and(owner, NZ - 1)
@@ -125,18 +134,24 @@
 
     pl.semaphore_wait(barrier, NZ - 1 + len(XY) + 1)
 
-    z_ids = []
     for s, dz in enumerate(ORDER):
         if dz:
-            z_ids.append(pltpu.make_async_remote_copy(
-                src_ref=ids_z.at[s], dst_ref=got_z.at[s], send_sem=z_send.at[s], recv_sem=z_recv.at[s],
-                device_id=z_peer((my_z - dz + NZ) % NZ), device_id_type=MESH))
-            z_ids[-1].start()
+            pltpu.make_async_remote_copy(
+                src_ref=ids_z.at[s], dst_ref=got_z.at[s], send_sem=z_send, recv_sem=z_recv,
+                device_id=z_peer((my_z - dz + NZ) % NZ), device_id_type=MESH).start()
         else:
             got_z[s] = ids_z[s]
 
-    for copy in z_ids:
-        copy.wait_recv()
+    def event_rows(first):
+        rows = pl.ds(first, HALF // 2)
+        pre = dot(hist_v[rows, :], we_v[...])
+        states_v[rows, :] = (hist_v[rows, :].astype(F32) + jax.nn.gelu(pre)).astype(BF16)
+
+    load_hist.wait()
+    load_we.wait()
+    event_rows(0)
+
+    drain(got_z.at[pl.ds(0, NZ - 1)], z_recv)
     turn[...] = jnp.zeros_like(turn)
     for s in range(NZ):
         turn[s * CAP:(s + 1) * CAP, :] = got_z[s, 0:CAP, :]
@@ -145,13 +160,11 @@
     over = jnp.max(got_z[:, CAP, :], axis=0, keepdims=True)
     for n in range(NYX):
         ids_xy[n] = jnp.where(iota((8, 128), 0) == 0, turned[n:n + 1, :], over)
-    xy_ids = []
-    for n, (dy, dx) in enumerate(XY):
+    for dy, dx in XY:
         target = xy_index(dy, dx)
-        xy_ids.append(pltpu.make_async_remote_copy(
-            src_ref=ids_xy.at[target], dst_ref=got_xy.at[my_yx], send_sem=xy_send.at[n], recv_sem=xy_recv.at[n],
-            device_id=xy_peer(target), device_id_type=MESH))
-        xy_ids[-1].start()
+        pltpu.make_async_remote_copy(
+            src_ref=ids_xy.at[target], dst_ref=got_xy.at[my_yx], send_sem=xy_send, recv_sem=xy_recv,
+            device_id=xy_peer(target), device_id_type=MESH).start()
     got_xy[my_yx] = ids_xy[my_yx]
 
     for g in range(NGROUP):
@@ -160,8 +173,9 @@
                 asked[g * GROUP:(g + 1) * GROUP, n:n + 1], (GROUP, 128))
         pos_row[g] = jnp.transpose(col[...])
 
-    for copy in xy_ids:
-        copy.wait_recv()
+    event_rows(HALF // 2)
+
+    drain(got_xy.at[pl.ds(0, NYX - 1)], xy_recv)
     turn[...] = jnp.zeros_like(turn)
     for n in range(NYX):
         turn[n:n + 1, :] = got_xy[n, 0:1, :]
@@ -169,7 +183,6 @@
     columns = jnp.bitwise_and(jnp.transpose(turn[...]).astype(I32), 8191)
     load_table.wait()
 
-    xy_rows = []
     lanes = iota((1, 128), 1) + 1
     chunk = 1024
     for g in range(NGROUP):
@@ -183,27 +196,17 @@
             term = dot(onehot[...], table_v[first:first + chunk, :])
             total = term if total is None else total + term
         rows_xy[g] = total.astype(BF16).reshape(NYX, GROUP, E)
-        for n, (dy, dx) in enumerate(XY):
+        for dy, dx in XY:
             target = xy_index(dy, dx)
-            xy_rows.append(pltpu.make_async_remote_copy(
+            pltpu.make_async_remote_copy(
                 src_ref=rows_xy.at[g, target], dst_ref=back_xy.at[g, my_yx],
-                send_sem=rxy_send.at[g, n], recv_sem=rxy_recv.at[g, n],
-                device_id=xy_peer(target), device_id_type=MESH))
-            xy_rows[-1].start()
+                send_sem=rxy_send, recv_sem=rxy_recv.at[g],
+                device_id=xy_peer(target), device_id_type=MESH).start()
         back_xy[g, my_yx] = rows_xy[g, my_yx]
-
-    load_hist.wait()
-    load_we.wait()
-    for first in range(0, HALF, 256):
-        events = hist_v[first:first + 256, :]
-        pre = dot(events, we_v[...])
-        states_v[first:first + 256, :] = (events.astype(F32) + jax.nn.gelu(pre)).astype(BF16)
-
-    z_rows = []
 
     def z_copy(s, src, dst, plane):
         return pltpu.make_async_remote_copy(
-            src_ref=src, dst_ref=dst, send_sem=rz_send.at[s], recv_sem=rz_recv.at[s],
+            src_ref=src, dst_ref=dst, send_sem=rz_send, recv_sem=rz_recv.at[s],
             device_id=z_peer(plane), device_id_type=MESH)
 
     def forward(s):
@@ -220,14 +223,12 @@
             total = term if total is None else total + term
         if ORDER[s]:
             rows_z[s] = total.astype(BF16)
-            z_rows.append(z_copy(s, rows_z.at[s], back_z.at[s], (my_z + ORDER[s]) % NZ))
-            z_rows[-1].start()
+            z_copy(s, rows_z.at[s], back_z.at[s], (my_z + ORDER[s]) % NZ).start()
         else:
             back_z[s] = total.astype(BF16)
 
     def forward_group(g):
-        for copy in xy_rows[g * len(XY):(g + 1) * len(XY)]:
-            copy.wait_recv()
+        drain(back_xy.at[g, pl.ds(0, NYX - 1)], rxy_recv.at[g])
         for s in range(NZ):
             if g * GROUP < (s + 1) * CAP <= (g + 1) * GROUP:
                 forward(s)
@@ -241,10 +242,11 @@
         device_id=other, device_id_type=MESH)
     kv_copy.start()
 
+    load_query.wait()
     scale = 1.0 / math.sqrt(HEAD)
     length = len_ref[0]
     of_head = (iota((16, D), 1) // HEAD) == iota((16, D), 0)
-    queries = jnp.where(of_head, query_ref[...].astype(F32).reshape(1, D), 0.0).astype(BF16)
+    queries = jnp.where(of_head, query_v[...].astype(F32).reshape(1, D), 0.0).astype(BF16)
     events = section * HALF + iota((1, HALF), 1)
     pool_score = jnp.where(events < length, dot_nt(queries, states_v[...]) * scale, MASKED)
     pool_max = jnp.max(pool_score, axis=-1, keepdims=True)
@@ -264,7 +266,6 @@
     pool_copy.start()
 
     forward_group(1)
-    forward_group(2)
 
     pool_copy.wait_recv()
     mine, theirs = pool_mine[...], pool_other[...]
@@ -275,9 +276,12 @@
     state = (first[0:1] * first_scale + second[0:1] * second_scale) / (
         first[2:3] * first_scale + second[2:3] * second_scale)
     state = state.astype(BF16)
-    user_ref[...] = state
-    over_ref[...] = jnp.maximum(mine[3:4, 0:128], theirs[3:4, 0:128])
+    user_v[...] = state
+    over_v[...] = jnp.maximum(mine[3:4, 0:128], theirs[3:4, 0:128])
+    put_user = load(user_v, user_ref, 8)
+    put_over = load(over_v, over_ref, 9)
     load_wr.wait()
+    load_wout.wait()
     user_term = dot(jnp.broadcast_to(state, (16, D)), wr_v[2 * E:, :])[0:1]
     kv_copy.wait_recv()
     for k in range(2):
@@ -286,6 +290,8 @@
             values_v[h, k * HALF:(k + 1) * HALF, 0:HEAD] = kv_v[k, :, E + h * HEAD:E + (h + 1) * HEAD]
             values_v[h, k * HALF:(k + 1) * HALF, HEAD:] = jnp.ones((HALF, HEAD), BF16)
     bias = jnp.where(iota((1, 2 * HALF), 1) < length, 0.0, MASKED)
+
+    forward_group(2)
 
     pair = 2 * cap_rows
 
@@ -316,7 +322,7 @@
             parts.append((early + late).astype(BF16))
         attended = jnp.concatenate(parts, axis=-1)
         hidden = dot(rows, wr_v[0:E, :]) + dot(attended, wr_v[E:2 * E, :]) + user_term
-        score = jnp.sum(jnp.maximum(hidden, 0.0) * wout_ref[...], axis=-1, keepdims=True)
+        score = jnp.sum(jnp.maximum(hidden, 0.0) * wout_v[...].reshape(1, E), axis=-1, keepdims=True)
         mine = (iota((pair, SLOTS), 0) + step * pair) == candidate
         return so_far + jnp.sum(jnp.where(mine, score, 0.0), axis=0, keepdims=True)
 
@@ -324,8 +330,14 @@
     live = section * SLOTS + iota((1, SLOTS), 1) < count_ref[0]
     scores_ref[...] = jnp.where(live, found, 0.0)
 
-    for copy in z_ids + xy_ids + xy_rows + z_rows + [kv_copy, pool_copy]:
-        copy.wait_send()
+    drain(ids_z.at[pl.ds(0, NZ - 1)], z_send)
+    drain(ids_xy.at[pl.ds(0, NYX - 1)], xy_send)
+    drain(rows_xy.at[:, pl.ds(0, NYX - 1)], rxy_send)
+    drain(rows_z.at[pl.ds(0, NZ - 1)], rz_send)
+    kv_copy.wait_send()
+    pool_copy.wait_send()
+    put_user.wait()
+    put_over.wait()
 
 
 def fetch_and_rank(cap_rows, collective_id, hist_len, cand_ids, cand_count, pool_query, w_out, history, table,
@@ -335,6 +347,8 @@
     anywhere = pl.BlockSpec(memory_space=pl.ANY)
     dma = pltpu.SemaphoreType.DMA
     scratch = [
+        pltpu.VMEM((1, SLOTS), I32), pltpu.VMEM((D,), BF16), pltpu.VMEM((E,), F32),
+        pltpu.VMEM((1, D), BF16), pltpu.VMEM((1, 128), F32),
         pltpu.VMEM((HALF, D), BF16), pltpu.VMEM((ROWS, E), BF16), pltpu.VMEM((D, D), BF16),
         pltpu.VMEM((D, 2 * E), BF16), pltpu.VMEM((2 * E + D, E), BF16), pltpu.VMEM((HALF, D), BF16),
         pltpu.VMEM((2, HALF, 2 * E), BF16),
@@ -346,22 +360,20 @@
         pltpu.VMEM((NZ, cap_rows, E), BF16), pltpu.VMEM((NZ, cap_rows, E), BF16),
         pltpu.VMEM((8, D), F32), pltpu.VMEM((8, D), F32),
         pltpu.VMEM((E, 2 * HALF), BF16), pltpu.VMEM((E // HEAD, 2 * HALF, 2 * HEAD), BF16),
-        dma((5,)), dma((NZ,)), dma((NZ,)), dma((len(XY),)), dma((len(XY),)), dma((NZ,)), dma((NZ,)),
-        dma((NGROUP, len(XY))), dma((NGROUP, len(XY))), dma((2,)), dma((2,)),
+        dma((10,)), dma, dma, dma, dma, dma, dma((NZ,)), dma, dma((NGROUP,)), dma((2,)), dma((2,)),
     ]
     return pl.pallas_call(
         functools.partial(kernel, cap_rows),
         out_shape=(
             jax.ShapeDtypeStruct((1, SLOTS), F32), jax.ShapeDtypeStruct((1, D), BF16),
             jax.ShapeDtypeStruct((1, 128), F32)),
-        in_specs=[vmem, smem, smem, vmem, vmem] + [anywhere] * 5,
-        out_specs=(vmem, vmem, vmem),
+        in_specs=[smem, smem] + [anywhere] * 8,
+        out_specs=(vmem, anywhere, anywhere),
         scratch_shapes=scratch,
         compiler_params=pltpu.CompilerParams(
             collective_id=collective_id, has_side_effects=True, vmem_limit_bytes=60 * 1024 * 1024),
         name="fetch_and_rank",
-    )(cand_ids, hist_len, cand_count, pool_query, w_out.reshape(1, E), history, table, w_event, w_kv,
-      w_rank)
+    )(hist_len, cand_count, cand_ids, pool_query, w_out, history, table, w_event, w_kv, w_rank)
 
 
 def on_device(

time: 48.1 us -> 45.1 us (0.938)
  the two profiles are of different devices: /device:TPU:8 before, /device:TPU:1 now
where the time goes in v3:
time: 45.1 us; the launch traced here: 45 us
  Pallas kernels  41 us (91%)
  between operations  2.66 us (6%)
  local copies, waits for them, and re-layouts  1.18 us (3%)
    pallas_call x1, Pallas kernels, fetch_and_rank(): pl.pallas_call(functools.partial(kernel, cap_rows), out_shape=(jax.ShapeD...  41 us
    unnamed x14, local copies, waits for them, and re-layouts  1.18 us

profile of v3, /device:TPU:1, one launch (start us, length us, event | category | flops | bytes accessed | tf_op | source)
XLA Modules:
  0.0 45.0 jit_solution(13578894727436736070)
XLA Ops:
  1.9 0.0 copy-start
  1.9 0.0 copy-start.1
  1.9 0.0 copy-start.2
  2.0 0.0 copy-start.3
  2.0 0.0 copy-start.4
  2.0 41.0 %fetch_and_rank.3 = (f32[1,384]{1,0:T(1,128)S(1)}, bf16[1,1024]{1,0:T(2,128)(2,1)}, f32[1,128]{1,0:T(1,128)}) custom-call(s32[1]{0:T(128)S(6)} %copy.16.len_ref, s32[1]{0:T(128)S(6)} %copy.17.count_ref, s32[1,384]{1,0:T(1,128)} %cand_ids.1, bf16[1024]{0:T(1024)(128)(2,1)} %pool_query.1, f32[512]{0:T(512)} %w_out.1, bf16[1,512,1024]{2,1,0:T(8,128)(2,1)} %history.1, ...), custom_call_target="tpu_custom_call" | custom-call | tf_op jit(solution)/shard_map/fetch_and_rank/pallas_call | solution.py:365
  43.6 0.0 copy-done
  43.6 0.0 copy-done.1
  43.6 0.0 copy-done.2
  43.6 0.0 copy-done.3
  43.7 0.0 copy-done.4
  43.7 0.0 copy-start.5
  43.7 0.2 conditional.1
  43.9 0.6 %copy.18 = f32[1,384]{1,0:T(1,128)} copy(f32[1,384]{1,0:T(1,128)S(1)} %get-tuple-element.47) | data formatting | bytes 3072
  44.4 0.0 copy-done.5
  44.4 0.6 %copy.19 = bf16[1,1024]{1,0:T(2,128)(2,1)} copy(bf16[1,1024]{1,0:T(2,128)(2,1)S(1)} %copy-done.5) | data formatting | bytes 4096
Async XLA Ops:
  1.9 41.7 %copy-start = (bf16[1024,1024]{1,0:T(8,128)(2,1)S(1)}, bf16[1024,1024]{1,0:T(8,128)(2,1)}, u32[]{:S(2)}) copy-start(bf16[1024,1024]{1,0:T(8,128)(2,1)} %w_event.1) | copy-start | bytes 6291460
  1.9 41.7 %copy-start.1 = (bf16[1,512,1024]{2,1,0:T(8,128)(2,1)S(1)}, bf16[1,512,1024]{2,1,0:T(8,128)(2,1)}, u32[]{:S(2)}) copy-start(bf16[1,512,1024]{2,1,0:T(8,128)(2,1)} %history.1) | copy-start | bytes 3145732
  1.9 41.7 %copy-start.2 = (bf16[1024]{0:T(1024)(128)(2,1)S(1)}, bf16[1024]{0:T(1024)(128)(2,1)}, u32[]{:S(2)}) copy-start(bf16[1024]{0:T(1024)(128)(2,1)} %pool_query.1) | copy-start | bytes 6148
  2.0 41.7 %copy-start.3 = (f32[512]{0:T(512)S(1)}, f32[512]{0:T(512)}, u32[]{:S(2)}) copy-start(f32[512]{0:T(512)} %w_out.1) | copy-start | bytes 6148
  2.0 41.7 %copy-start.4 = (s32[1,384]{1,0:T(1,128)S(1)}, s32[1,384]{1,0:T(1,128)}, u32[]{:S(2)}) copy-start(s32[1,384]{1,0:T(1,128)} %cand_ids.1) | copy-start | bytes 4612
  43.7 0.8 %copy-start.5 = (bf16[1,1024]{1,0:T(2,128)(2,1)S(1)}, bf16[1,1024]{1,0:T(2,128)(2,1)}, u32[]{:S(2)}) copy-start(bf16[1,1024]{1,0:T(2,128)(2,1)} %get-tuple-element.46) | copy-start | bytes 6148

commit v4 on v3

--- a/solution.py
+++ b/solution.py
@@ -19,15 +19,15 @@
 CAP = 6
 ORDER = (4, 5, 3, 6, 2, 1, 7, 0)
 ROOM = 56
-GROUP = 16
-NGROUP = NZ * CAP // GROUP
+GROUPS = (8, 16, 24)
+STARTS = tuple(sum(GROUPS[:g]) for g in range(len(GROUPS)))
 ROWS = 4096
 E = 512
 D = 1024
 HALF = 512
 SLOTS = 384
 MASKED = -1e30
-XY = tuple((dy, dx) for dy in range(NY) for dx in range(NX) if (dy, dx) != (0, 0))
+XY = tuple((dy, dx) for dy in (2, 1, 3, 0) for dx in (2, 1, 3, 0) if (dy, dx) != (0, 0))
 
 
 def iota(shape, axis):
@@ -48,7 +48,7 @@
     history, table, w_event, w_kv, w_rank,
     scores_ref, user_ref, over_ref,
     ids_v, query_v, wout_v, user_v, over_v, hist_v, table_v, we_v, wkv_v, wr_v, states_v, kv_v,
-    ids_z, got_z, turn, ids_xy, got_xy, col, pos_row, onehot,
+    ids_z, got_z, turn, ids_xy, got_xy, col, pos_rows, onehot,
     rows_xy, back_xy, rows_z, back_z, pool_mine, pool_other, keys_v, values_v,
     local_sem, z_send, z_recv, xy_send, xy_recv, rz_send, rz_recv, rxy_send, rxy_recv, pair_send, pair_recv,
 ):
@@ -167,11 +167,10 @@
             device_id=xy_peer(target), device_id_type=MESH).start()
     got_xy[my_yx] = ids_xy[my_yx]
 
-    for g in range(NGROUP):
+    for size, start, pos_row in zip(GROUPS, STARTS, pos_rows):
         for n in range(NYX):
-            col[n * GROUP:(n + 1) * GROUP, :] = jnp.broadcast_to(
-                asked[g * GROUP:(g + 1) * GROUP, n:n + 1], (GROUP, 128))
-        pos_row[g] = jnp.transpose(col[...])
+            col[n * size:(n + 1) * size, :] = jnp.broadcast_to(asked[start:start + size, n:n + 1], (size, 128))
+        pos_row[...] = jnp.transpose(col[0:NYX * size, :])
 
     event_rows(HALF // 2)
 
@@ -185,24 +184,25 @@
 
     lanes = iota((1, 128), 1) + 1
     chunk = 1024
-    for g in range(NGROUP):
+    for g, (size, start) in enumerate(zip(GROUPS, STARTS)):
+        count = NYX * size
         wants = jnp.concatenate(
-            [jnp.broadcast_to(columns[g * GROUP:(g + 1) * GROUP, n:n + 1], (GROUP, 128)) for n in range(NYX)], axis=0)
+            [jnp.broadcast_to(columns[start:start + size, n:n + 1], (size, 128)) for n in range(NYX)], axis=0)
         total = None
         for first in range(0, ROWS, chunk):
             for block in range(0, chunk, 128):
-                onehot[:, block:block + 128] = jnp.where(
+                onehot[0:count, block:block + 128] = jnp.where(
                     wants == lanes + (first + block), 1.0, 0.0).astype(BF16)
-            term = dot(onehot[...], table_v[first:first + chunk, :])
+            term = dot(onehot[0:count, :], table_v[first:first + chunk, :])
             total = term if total is None else total + term
-        rows_xy[g] = total.astype(BF16).reshape(NYX, GROUP, E)
+        rows_xy[g][...] = total.astype(BF16).reshape(NYX, size, E)
         for dy, dx in XY:
             target = xy_index(dy, dx)
             pltpu.make_async_remote_copy(
-                src_ref=rows_xy.at[g, target], dst_ref=back_xy.at[g, my_yx],
-                send_sem=rxy_send, recv_sem=rxy_recv.at[g],
+                src_ref=rows_xy[g].at[target], dst_ref=back_xy[g].at[my_yx],
+                send_sem=rxy_send.at[g], recv_sem=rxy_recv.at[g],
                 device_id=xy_peer(target), device_id_type=MESH).start()
-        back_xy[g, my_yx] = rows_xy[g, my_yx]
+        back_xy[g][my_yx] = rows_xy[g][my_yx]
 
     def z_copy(s, src, dst, plane):
         return pltpu.make_async_remote_copy(
@@ -211,15 +211,15 @@
 
     def forward(s):
         total = None
-        for g in range(NGROUP):
-            if (s + 1) * CAP <= g * GROUP or s * CAP >= (g + 1) * GROUP:
+        for g, (size, start) in enumerate(zip(GROUPS, STARTS)):
+            if (s + 1) * CAP <= start or s * CAP >= start + size:
                 continue
-            entries = pos_row[g][0:cap_rows, :].astype(I32)
-            here = jnp.bitwise_and(iota((1, NYX * GROUP), 1), GROUP - 1) + g * GROUP
+            entries = pos_rows[g][0:cap_rows, :].astype(I32)
+            here = lax.rem(iota((1, NYX * size), 1), size) + start
             mine = (here >= s * CAP) & (here < (s + 1) * CAP)
             filled = jnp.bitwise_and(entries, 8191) > 0
-            pick = (lax.shift_right_logical(entries, 13) == iota((cap_rows, NYX * GROUP), 0)) & filled & mine
-            term = dot(pick.astype(F32).astype(BF16), back_xy[g].reshape(NYX * GROUP, E))
+            pick = (lax.shift_right_logical(entries, 13) == iota((cap_rows, NYX * size), 0)) & filled & mine
+            term = dot(pick.astype(F32).astype(BF16), back_xy[g][...].reshape(NYX * size, E))
             total = term if total is None else total + term
         if ORDER[s]:
             rows_z[s] = total.astype(BF16)
@@ -228,9 +228,9 @@
             back_z[s] = total.astype(BF16)
 
     def forward_group(g):
-        drain(back_xy.at[g, pl.ds(0, NYX - 1)], rxy_recv.at[g])
+        drain(back_xy[g].at[pl.ds(0, NYX - 1)], rxy_recv.at[g])
         for s in range(NZ):
-            if g * GROUP < (s + 1) * CAP <= (g + 1) * GROUP:
+            if STARTS[g] < (s + 1) * CAP <= STARTS[g] + GROUPS[g]:
                 forward(s)
 
     forward_group(0)
@@ -293,15 +293,15 @@
 
     forward_group(2)
 
-    pair = 2 * cap_rows
+    batch = 4 * cap_rows
 
     def attend(step, so_far):
-        for s in (2 * step, 2 * step + 1):
+        for s in (4 * step, 4 * step + 1, 4 * step + 2, 4 * step + 3):
             @pl.when(s != NZ - 1)
             def _():
                 z_copy(s, rows_z.at[s], back_z.at[s], my_z).wait_recv()
 
-        rows = back_z[pl.ds(2 * step, 2)].reshape(pair, E)
+        rows = back_z[pl.ds(4 * step, 4)].reshape(batch, E)
 
         def scores(h):
             return dot(rows[:, h * HEAD:(h + 1) * HEAD], keys_v[h * HEAD:(h + 1) * HEAD, :])
@@ -323,16 +323,17 @@
         attended = jnp.concatenate(parts, axis=-1)
         hidden = dot(rows, wr_v[0:E, :]) + dot(attended, wr_v[E:2 * E, :]) + user_term
         score = jnp.sum(jnp.maximum(hidden, 0.0) * wout_v[...].reshape(1, E), axis=-1, keepdims=True)
-        mine = (iota((pair, SLOTS), 0) + step * pair) == candidate
+        mine = (iota((batch, SLOTS), 0) + step * batch) == candidate
         return so_far + jnp.sum(jnp.where(mine, score, 0.0), axis=0, keepdims=True)
 
-    found = lax.fori_loop(0, NZ // 2, attend, jnp.zeros((1, SLOTS), F32))
+    found = lax.fori_loop(0, NZ // 4, attend, jnp.zeros((1, SLOTS), F32))
     live = section * SLOTS + iota((1, SLOTS), 1) < count_ref[0]
     scores_ref[...] = jnp.where(live, found, 0.0)
 
     drain(ids_z.at[pl.ds(0, NZ - 1)], z_send)
     drain(ids_xy.at[pl.ds(0, NYX - 1)], xy_send)
-    drain(rows_xy.at[:, pl.ds(0, NYX - 1)], rxy_send)
+    for g in range(len(GROUPS)):
+        drain(rows_xy[g].at[pl.ds(0, NYX - 1)], rxy_send.at[g])
     drain(rows_z.at[pl.ds(0, NZ - 1)], rz_send)
     kv_copy.wait_send()
     pool_copy.wait_send()
@@ -354,13 +355,15 @@
         pltpu.VMEM((2, HALF, 2 * E), BF16),
         pltpu.VMEM((NZ, 8, 128), F32), pltpu.VMEM((NZ, 8, 128), F32), pltpu.VMEM((128, 128), F32),
         pltpu.VMEM((NYX, 8, 128), F32), pltpu.VMEM((NYX, 8, 128), F32),
-        pltpu.VMEM((NYX * GROUP, 128), F32), pltpu.VMEM((NGROUP, 128, NYX * GROUP), F32),
-        pltpu.VMEM((NYX * GROUP, 1024), BF16),
-        pltpu.VMEM((NGROUP, NYX, GROUP, E), BF16), pltpu.VMEM((NGROUP, NYX, GROUP, E), BF16),
+        pltpu.VMEM((NYX * max(GROUPS), 128), F32),
+        [pltpu.VMEM((128, NYX * size), F32) for size in GROUPS],
+        pltpu.VMEM((NYX * max(GROUPS), 1024), BF16),
+        [pltpu.VMEM((NYX, size, E), BF16) for size in GROUPS], [pltpu.VMEM((NYX, size, E), BF16) for size in GROUPS],
         pltpu.VMEM((NZ, cap_rows, E), BF16), pltpu.VMEM((NZ, cap_rows, E), BF16),
         pltpu.VMEM((8, D), F32), pltpu.VMEM((8, D), F32),
         pltpu.VMEM((E, 2 * HALF), BF16), pltpu.VMEM((E // HEAD, 2 * HALF, 2 * HEAD), BF16),
-        dma((10,)), dma, dma, dma, dma, dma, dma((NZ,)), dma, dma((NGROUP,)), dma((2,)), dma((2,)),
+        dma((10,)), dma, dma, dma, dma, dma, dma((NZ,)),
+        dma((len(GROUPS),)), dma((len(GROUPS),)), dma((2,)), dma((2,)),
     ]
     return pl.pallas_call(
         functools.partial(kernel, cap_rows),

time: 45.1 us -> 43.5 us (0.965)
  Pallas kernels: 41 us -> 39.4 us
    pallas_call x1, Pallas kernels: 41 us -> 39.4 us  [fetch_and_rank(): pl.pallas_call(functools.partial(kernel, cap_rows), out_shape=(jax.ShapeD...]
where the time goes in v4:
time: 43.5 us; the launch traced here: 43.4 us
  Pallas kernels  39.4 us (91%)
  between operations  2.66 us (6%)
  local copies, waits for them, and re-layouts  1.18 us (3%)
    pallas_call x1, Pallas kernels, fetch_and_rank(): pl.pallas_call(functools.partial(kernel, cap_rows), out_shape=(jax.ShapeD...  39.4 us
    unnamed x14, local copies, waits for them, and re-layouts  1.18 us

profile of v4, /device:TPU:1, one launch (start us, length us, event | category | flops | bytes accessed | tf_op | source)
XLA Modules:
  0.0 43.4 jit_solution(10230594110397940261)
XLA Ops:
  1.9 0.0 copy-start
  1.9 0.0 copy-start.1
  1.9 0.0 copy-start.2
  2.0 0.0 copy-start.3
  2.0 0.0 copy-start.4
  2.0 39.4 %fetch_and_rank.3 = (f32[1,384]{1,0:T(1,128)S(1)}, bf16[1,1024]{1,0:T(2,128)(2,1)}, f32[1,128]{1,0:T(1,128)}) custom-call(s32[1]{0:T(128)S(6)} %copy.16.len_ref, s32[1]{0:T(128)S(6)} %copy.17.count_ref, s32[1,384]{1,0:T(1,128)} %cand_ids.1, bf16[1024]{0:T(1024)(128)(2,1)} %pool_query.1, f32[512]{0:T(512)} %w_out.1, bf16[1,512,1024]{2,1,0:T(8,128)(2,1)} %history.1, ...), custom_call_target="tpu_custom_call" | custom-call | tf_op jit(solution)/shard_map/fetch_and_rank/pallas_call | solution.py:368
  42.0 0.0 copy-done
  42.0 0.0 copy-done.1
  42.0 0.0 copy-done.2
  42.0 0.0 copy-done.3
  42.0 0.0 copy-done.4
  42.0 0.0 copy-start.5
  42.0 0.2 conditional.1
  42.2 0.6 %copy.18 = f32[1,384]{1,0:T(1,128)} copy(f32[1,384]{1,0:T(1,128)S(1)} %get-tuple-element.47) | data formatting | bytes 3072
  42.8 0.0 copy-done.5
  42.8 0.6 %copy.19 = bf16[1,1024]{1,0:T(2,128)(2,1)} copy(bf16[1,1024]{1,0:T(2,128)(2,1)S(1)} %copy-done.5) | data formatting | bytes 4096
Async XLA Ops:
  1.9 40.0 %copy-start = (bf16[1024,1024]{1,0:T(8,128)(2,1)S(1)}, bf16[1024,1024]{1,0:T(8,128)(2,1)}, u32[]{:S(2)}) copy-start(bf16[1024,1024]{1,0:T(8,128)(2,1)} %w_event.1) | copy-start | bytes 6291460
  1.9 40.0 %copy-start.1 = (bf16[1,512,1024]{2,1,0:T(8,128)(2,1)S(1)}, bf16[1,512,1024]{2,1,0:T(8,128)(2,1)}, u32[]{:S(2)}) copy-start(bf16[1,512,1024]{2,1,0:T(8,128)(2,1)} %history.1) | copy-start | bytes 3145732
  1.9 40.0 %copy-start.2 = (bf16[1024]{0:T(1024)(128)(2,1)S(1)}, bf16[1024]{0:T(1024)(128)(2,1)}, u32[]{:S(2)}) copy-start(bf16[1024]{0:T(1024)(128)(2,1)} %pool_query.1) | copy-start | bytes 6148
  2.0 40.0 %copy-start.3 = (f32[512]{0:T(512)S(1)}, f32[512]{0:T(512)}, u32[]{:S(2)}) copy-start(f32[512]{0:T(512)} %w_out.1) | copy-start | bytes 6148
  2.0 40.0 %copy-start.4 = (s32[1,384]{1,0:T(1,128)S(1)}, s32[1,384]{1,0:T(1,128)}, u32[]{:S(2)}) copy-start(s32[1,384]{1,0:T(1,128)} %cand_ids.1) | copy-start | bytes 4612
  42.0 0.8 %copy-start.5 = (bf16[1,1024]{1,0:T(2,128)(2,1)S(1)}, bf16[1,1024]{1,0:T(2,128)(2,1)}, u32[]{:S(2)}) copy-start(bf16[1,1024]{1,0:T(2,128)(2,1)} %get-tuple-element.46) | copy-start | bytes 6148

commit v5 on v4

--- a/solution.py
+++ b/solution.py
@@ -78,11 +78,12 @@
         return (section, yx * NZ + my_z)
 
     other = (1 - section, item)
+    peers = [xy_index(dy, dx) for dy, dx in XY]
     barrier = pltpu.get_barrier_semaphore()
     for dz in range(1, NZ):
         pl.semaphore_signal(barrier, inc=1, device_id=z_peer((my_z + dz) % NZ), device_id_type=MESH)
-    for dy, dx in XY:
-        pl.semaphore_signal(barrier, inc=1, device_id=xy_peer(xy_index(dy, dx)), device_id_type=MESH)
+    for target in peers:
+        pl.semaphore_signal(barrier, inc=1, device_id=xy_peer(target), device_id_type=MESH)
     pl.semaphore_signal(barrier, inc=1, device_id=other, device_id_type=MESH)
 
     load_hist = load(history.at[0], hist_v, 0)
@@ -147,10 +148,6 @@
         pre = dot(hist_v[rows, :], we_v[...])
         states_v[rows, :] = (hist_v[rows, :].astype(F32) + jax.nn.gelu(pre)).astype(BF16)
 
-    load_hist.wait()
-    load_we.wait()
-    event_rows(0)
-
     drain(got_z.at[pl.ds(0, NZ - 1)], z_recv)
     turn[...] = jnp.zeros_like(turn)
     for s in range(NZ):
@@ -160,8 +157,7 @@
     over = jnp.max(got_z[:, CAP, :], axis=0, keepdims=True)
     for n in range(NYX):
         ids_xy[n] = jnp.where(iota((8, 128), 0) == 0, turned[n:n + 1, :], over)
-    for dy, dx in XY:
-        target = xy_index(dy, dx)
+    for target in peers:
         pltpu.make_async_remote_copy(
             src_ref=ids_xy.at[target], dst_ref=got_xy.at[my_yx], send_sem=xy_send, recv_sem=xy_recv,
             device_id=xy_peer(target), device_id_type=MESH).start()
@@ -172,6 +168,9 @@
             col[n * size:(n + 1) * size, :] = jnp.broadcast_to(asked[start:start + size, n:n + 1], (size, 128))
         pos_row[...] = jnp.transpose(col[0:NYX * size, :])
 
+    load_hist.wait()
+    load_we.wait()
+    event_rows(0)
     event_rows(HALF // 2)
 
     drain(got_xy.at[pl.ds(0, NYX - 1)], xy_recv)
@@ -183,7 +182,7 @@
     load_table.wait()
 
     lanes = iota((1, 128), 1) + 1
-    chunk = 1024
+    chunk = 512
     for g, (size, start) in enumerate(zip(GROUPS, STARTS)):
         count = NYX * size
         wants = jnp.concatenate(
@@ -191,13 +190,12 @@
         total = None
         for first in range(0, ROWS, chunk):
             for block in range(0, chunk, 128):
-                onehot[0:count, block:block + 128] = jnp.where(
+                onehot[first // chunk, 0:count, block:block + 128] = jnp.where(
                     wants == lanes + (first + block), 1.0, 0.0).astype(BF16)
-            term = dot(onehot[0:count, :], table_v[first:first + chunk, :])
+            term = dot(onehot[first // chunk, 0:count, :], table_v[first:first + chunk, :])
             total = term if total is None else total + term
         rows_xy[g][...] = total.astype(BF16).reshape(NYX, size, E)
-        for dy, dx in XY:
-            target = xy_index(dy, dx)
+        for target in peers:
             pltpu.make_async_remote_copy(
                 src_ref=rows_xy[g].at[target], dst_ref=back_xy[g].at[my_yx],
                 send_sem=rxy_send.at[g], recv_sem=rxy_recv.at[g],
@@ -357,7 +355,7 @@
         pltpu.VMEM((NYX, 8, 128), F32), pltpu.VMEM((NYX, 8, 128), F32),
         pltpu.VMEM((NYX * max(GROUPS), 128), F32),
         [pltpu.VMEM((128, NYX * size), F32) for size in GROUPS],
-        pltpu.VMEM((NYX * max(GROUPS), 1024), BF16),
+        pltpu.VMEM((ROWS // 512, NYX * max(GROUPS), 512), BF16),
         [pltpu.VMEM((NYX, size, E), BF16) for size in GROUPS], [pltpu.VMEM((NYX, size, E), BF16) for size in GROUPS],
         pltpu.VMEM((NZ, cap_rows, E), BF16), pltpu.VMEM((NZ, cap_rows, E), BF16),
         pltpu.VMEM((8, D), F32), pltpu.VMEM((8, D), F32),

time: 43.5 us -> 43.2 us (level)
  no operation moved by 1% of the time
where the time goes in v5:
time: 43.2 us; the launch traced here: 43 us
  Pallas kernels  39 us (90%)
  between operations  2.66 us (6%)
  local copies, waits for them, and re-layouts  1.18 us (3%)
    pallas_call x1, Pallas kernels, fetch_and_rank(): pl.pallas_call(functools.partial(kernel, cap_rows), out_shape=(jax.ShapeD...  39 us
    unnamed x14, local copies, waits for them, and re-layouts  1.18 us

profile of v5, /device:TPU:1, one launch (start us, length us, event | category | flops | bytes accessed | tf_op | source)
XLA Modules:
  0.0 43.0 jit_solution(4228993493788499919)
XLA Ops:
  1.9 0.0 copy-start
  1.9 0.0 copy-start.1
  1.9 0.0 copy-start.2
  2.0 0.0 copy-start.3
  2.0 0.0 copy-start.4
  2.0 39.0 %fetch_and_rank.3 = (f32[1,384]{1,0:T(1,128)S(1)}, bf16[1,1024]{1,0:T(2,128)(2,1)}, f32[1,128]{1,0:T(1,128)}) custom-call(s32[1]{0:T(128)S(6)} %copy.16.len_ref, s32[1]{0:T(128)S(6)} %copy.17.count_ref, s32[1,384]{1,0:T(1,128)} %cand_ids.1, bf16[1024]{0:T(1024)(128)(2,1)} %pool_query.1, f32[512]{0:T(512)} %w_out.1, bf16[1,512,1024]{2,1,0:T(8,128)(2,1)} %history.1, ...), custom_call_target="tpu_custom_call" | custom-call | tf_op jit(solution)/shard_map/fetch_and_rank/pallas_call | solution.py:366
  41.6 0.0 copy-done
  41.6 0.0 copy-done.1
  41.7 0.0 copy-done.2
  41.7 0.0 copy-done.3
  41.7 0.0 copy-done.4
  41.7 0.0 copy-start.5
  41.7 0.2 conditional.1
  41.9 0.6 %copy.18 = f32[1,384]{1,0:T(1,128)} copy(f32[1,384]{1,0:T(1,128)S(1)} %get-tuple-element.47) | data formatting | bytes 3072
  42.5 0.0 copy-done.5
  42.5 0.6 %copy.19 = bf16[1,1024]{1,0:T(2,128)(2,1)} copy(bf16[1,1024]{1,0:T(2,128)(2,1)S(1)} %copy-done.5) | data formatting | bytes 4096
Async XLA Ops:
  1.9 39.7 %copy-start = (bf16[1024,1024]{1,0:T(8,128)(2,1)S(1)}, bf16[1024,1024]{1,0:T(8,128)(2,1)}, u32[]{:S(2)}) copy-start(bf16[1024,1024]{1,0:T(8,128)(2,1)} %w_event.1) | copy-start | bytes 6291460
  1.9 39.7 %copy-start.1 = (bf16[1,512,1024]{2,1,0:T(8,128)(2,1)S(1)}, bf16[1,512,1024]{2,1,0:T(8,128)(2,1)}, u32[]{:S(2)}) copy-start(bf16[1,512,1024]{2,1,0:T(8,128)(2,1)} %history.1) | copy-start | bytes 3145732
  1.9 39.7 %copy-start.2 = (bf16[1024]{0:T(1024)(128)(2,1)S(1)}, bf16[1024]{0:T(1024)(128)(2,1)}, u32[]{:S(2)}) copy-start(bf16[1024]{0:T(1024)(128)(2,1)} %pool_query.1) | copy-start | bytes 6148
  2.0 39.7 %copy-start.3 = (f32[512]{0:T(512)S(1)}, f32[512]{0:T(512)}, u32[]{:S(2)}) copy-start(f32[512]{0:T(512)} %w_out.1) | copy-start | bytes 6148
  2.0 39.7 %copy-start.4 = (s32[1,384]{1,0:T(1,128)S(1)}, s32[1,384]{1,0:T(1,128)}, u32[]{:S(2)}) copy-start(s32[1,384]{1,0:T(1,128)} %cand_ids.1) | copy-start | bytes 4612
  41.7 0.8 %copy-start.5 = (bf16[1,1024]{1,0:T(2,128)(2,1)S(1)}, bf16[1,1024]{1,0:T(2,128)(2,1)}, u32[]{:S(2)}) copy-start(bf16[1,1024]{1,0:T(2,128)(2,1)} %get-tuple-element.46) | copy-start | bytes 6148

commit v6 on v5

--- a/solution.py
+++ b/solution.py
@@ -290,6 +290,14 @@
     bias = jnp.where(iota((1, 2 * HALF), 1) < length, 0.0, MASKED)
 
     forward_group(2)
+    drain(ids_z.at[pl.ds(0, NZ - 1)], z_send)
+    drain(ids_xy.at[pl.ds(0, NYX - 1)], xy_send)
+    for g in range(len(GROUPS)):
+        drain(rows_xy[g].at[pl.ds(0, NYX - 1)], rxy_send.at[g])
+    kv_copy.wait_send()
+    pool_copy.wait_send()
+    put_user.wait()
+    put_over.wait()
 
     batch = 4 * cap_rows
 
@@ -328,15 +336,7 @@
     live = section * SLOTS + iota((1, SLOTS), 1) < count_ref[0]
     scores_ref[...] = jnp.where(live, found, 0.0)
 
-    drain(ids_z.at[pl.ds(0, NZ - 1)], z_send)
-    drain(ids_xy.at[pl.ds(0, NYX - 1)], xy_send)
-    for g in range(len(GROUPS)):
-        drain(rows_xy[g].at[pl.ds(0, NYX - 1)], rxy_send.at[g])
     drain(rows_z.at[pl.ds(0, NZ - 1)], rz_send)
-    kv_copy.wait_send()
-    pool_copy.wait_send()
-    put_user.wait()
-    put_over.wait()
 
 
 def fetch_and_rank(cap_rows, collective_id, hist_len, cand_ids, cand_count, pool_query, w_out, history, table,

time: 43.2 us -> 43.1 us (level)
  no operation moved by 1% of the time
where the time goes in v6:
time: 43.1 us; the launch traced here: 43 us
  Pallas kernels  39 us (90%)
  between operations  2.66 us (6%)
  local copies, waits for them, and re-layouts  1.18 us (3%)
    pallas_call x1, Pallas kernels, fetch_and_rank(): pl.pallas_call(functools.partial(kernel, cap_rows), out_shape=(jax.ShapeD...  39 us
    unnamed x14, local copies, waits for them, and re-layouts  1.18 us

profile of v6, /device:TPU:1, one launch (start us, length us, event | category | flops | bytes accessed | tf_op | source)
XLA Modules:
  0.0 43.0 jit_solution(882759609425708796)
XLA Ops:
  1.9 0.0 copy-start
  1.9 0.0 copy-start.1
  1.9 0.0 copy-start.2
  2.0 0.0 copy-start.3
  2.0 0.0 copy-start.4
  2.0 39.0 %fetch_and_rank.3 = (f32[1,384]{1,0:T(1,128)S(1)}, bf16[1,1024]{1,0:T(2,128)(2,1)}, f32[1,128]{1,0:T(1,128)}) custom-call(s32[1]{0:T(128)S(6)} %copy.16.len_ref, s32[1]{0:T(128)S(6)} %copy.17.count_ref, s32[1,384]{1,0:T(1,128)} %cand_ids.1, bf16[1024]{0:T(1024)(128)(2,1)} %pool_query.1, f32[512]{0:T(512)} %w_out.1, bf16[1,512,1024]{2,1,0:T(8,128)(2,1)} %history.1, ...), custom_call_target="tpu_custom_call" | custom-call | tf_op jit(solution)/shard_map/fetch_and_rank/pallas_call | solution.py:366
  41.6 0.0 copy-done
  41.6 0.0 copy-done.1
  41.6 0.0 copy-done.2
  41.6 0.0 copy-done.3
  41.7 0.0 copy-done.4
  41.7 0.0 copy-start.5
  41.7 0.2 conditional.1
  41.9 0.6 %copy.18 = f32[1,384]{1,0:T(1,128)} copy(f32[1,384]{1,0:T(1,128)S(1)} %get-tuple-element.47) | data formatting | bytes 3072
  42.4 0.0 copy-done.5
  42.4 0.6 %copy.19 = bf16[1,1024]{1,0:T(2,128)(2,1)} copy(bf16[1,1024]{1,0:T(2,128)(2,1)S(1)} %copy-done.5) | data formatting | bytes 4096
Async XLA Ops:
  1.9 39.7 %copy-start = (bf16[1024,1024]{1,0:T(8,128)(2,1)S(1)}, bf16[1024,1024]{1,0:T(8,128)(2,1)}, u32[]{:S(2)}) copy-start(bf16[1024,1024]{1,0:T(8,128)(2,1)} %w_event.1) | copy-start | bytes 6291460
  1.9 39.7 %copy-start.1 = (bf16[1,512,1024]{2,1,0:T(8,128)(2,1)S(1)}, bf16[1,512,1024]{2,1,0:T(8,128)(2,1)}, u32[]{:S(2)}) copy-start(bf16[1,512,1024]{2,1,0:T(8,128)(2,1)} %history.1) | copy-start | bytes 3145732
  1.9 39.7 %copy-start.2 = (bf16[1024]{0:T(1024)(128)(2,1)S(1)}, bf16[1024]{0:T(1024)(128)(2,1)}, u32[]{:S(2)}) copy-start(bf16[1024]{0:T(1024)(128)(2,1)} %pool_query.1) | copy-start | bytes 6148
  2.0 39.7 %copy-start.3 = (f32[512]{0:T(512)S(1)}, f32[512]{0:T(512)}, u32[]{:S(2)}) copy-start(f32[512]{0:T(512)} %w_out.1) | copy-start | bytes 6148
  2.0 39.7 %copy-start.4 = (s32[1,384]{1,0:T(1,128)S(1)}, s32[1,384]{1,0:T(1,128)}, u32[]{:S(2)}) copy-start(s32[1,384]{1,0:T(1,128)} %cand_ids.1) | copy-start | bytes 4612
  41.7 0.8 %copy-start.5 = (bf16[1,1024]{1,0:T(2,128)(2,1)S(1)}, bf16[1,1024]{1,0:T(2,128)(2,1)}, u32[]{:S(2)}) copy-start(bf16[1,1024]{1,0:T(2,128)(2,1)} %get-tuple-element.46) | copy-start | bytes 6148
